TPU v7x, 512 devices: a whole 4x4x16 slice. The times are simulated.
512 devices in a mesh: ctx: 64 (over x, z_hi, y), tp: 8 (over z_lo, core).
Axes of the slice: x: 4, y: 4, z: 16 (z_hi: 4, z_lo: 4; z = z_hi * 4 + z_lo), core: 2. Of those that a mesh axis runs over, the one named last changes fastest.
Arguments:
- query_branch: bfloat16 [12288, 2048], P('ctx', 'tp'), may hold values from -6 to 6
- key_branch: bfloat16 [12288, 2048], P('ctx', 'tp'), may hold values from -6 to 6
- value_branch: bfloat16 [12288, 2048], P('ctx', 'tp'), may hold values from -6 to 6
- spectrum: float32 [2, 128, 192, 2048], P(None, 'ctx', None, 'tp'), may hold values from -6 to 6
- skip_gain: float32 [2048], P('tp'), may hold values from -4 to 4
- out_weight: bfloat16 [2048, 4096], P('tp'), may hold values from -0.125 to 0.125
Outputs:
- layer_out: bfloat16 [12288, 4096], P('ctx', 'tp')
All inputs are finite; a program needn't handle non-finite values.
Results may differ from a plain program's by a relative error of at most 0.017.
Values may be sent and summed in bfloat16 or wider, within the bound.
No kernel may reach another device: no remote copies, remote signals or barrier semaphores. Data moves between devices by JAX's collectives and lax.ppermute only.
A program may use at most 64 MiB of HBM per device.

v0:
```python
import math

import jax
import jax.numpy as jnp
from jax import lax
from jax.sharding import PartitionSpec as P


def angle_tables(out_index, in_index, modulus):
    product = out_index[:, None] * in_index[None, :] % modulus
    angles = product.astype(jnp.float32) * (2.0 * math.pi / modulus)
    return (jnp.cos(angles), jnp.sin(angles))


def transform_middle(table, values):
    return jnp.einsum("ka,rac->rkc", table, values, precision=lax.Precision.HIGHEST)


def twist(real_part, imag_part, twist_cos, twist_sin, direction):
    new_real = real_part * twist_cos + direction * imag_part * twist_sin
    new_imag = imag_part * twist_cos - direction * real_part * twist_sin
    return (new_real, new_imag)


def spectral_step(
    real_part, imag_part, cos_tokens, sin_tokens, filter_real, filter_imag, transform
):
    forward_real = transform(cos_tokens, real_part) + transform(sin_tokens, imag_part)
    forward_imag = transform(cos_tokens, imag_part) - transform(sin_tokens, real_part)
    product_real = forward_real * filter_real - forward_imag * filter_imag
    product_imag = forward_real * filter_imag + forward_imag * filter_real
    inverse_real = transform(cos_tokens, product_real) - transform(sin_tokens, product_imag)
    inverse_imag = transform(cos_tokens, product_imag) + transform(sin_tokens, product_real)
    return (inverse_real, inverse_imag)


def sequence_path(mixed_in, spectrum, groups, position):
    tokens_here, channels = mixed_in.shape
    row_count = 2 * groups
    length = row_count * tokens_here
    col_count = tokens_here // groups
    local_rows = row_count // groups
    inverse_scale = 1.0 / length
    row_index = jnp.arange(row_count, dtype=jnp.int32)
    token_index = jnp.arange(tokens_here, dtype=jnp.int32)
    cos_rows, sin_rows = angle_tables(row_index, jnp.arange(groups, dtype=jnp.int32), row_count)
    col_index = position * col_count + jnp.arange(col_count, dtype=jnp.int32)
    twist_cos, twist_sin = angle_tables(row_index, col_index, length)
    flattened = (
        lax.all_to_all(
            mixed_in.reshape(1, groups, col_count, channels),
            "ctx",
            split_axis=1,
            concat_axis=0,
            tiled=True,
        )
        .reshape(groups, -1)
        .astype(jnp.float32)
    )
    real_part = jnp.dot(cos_rows, flattened, precision=lax.Precision.HIGHEST).reshape(
        row_count, col_count, -1
    )
    imag_part = -jnp.dot(sin_rows, flattened, precision=lax.Precision.HIGHEST).reshape(
        row_count, col_count, -1
    )
    real_part, imag_part = twist(
        real_part, imag_part, twist_cos[:, :, None], twist_sin[:, :, None], 1.0
    )
    spread = jnp.stack([real_part, imag_part])
    spectral = lax.all_to_all(spread, "ctx", split_axis=1, concat_axis=2, tiled=True)
    cos_tokens, sin_tokens = angle_tables(token_index, token_index, tokens_here)
    inverse_real, inverse_imag = spectral_step(
        spectral[0], spectral[1], cos_tokens, sin_tokens, spectrum[0], spectrum[1], transform_middle
    )
    freq_index = position * local_rows + jnp.arange(local_rows, dtype=jnp.int32)
    back_cos, back_sin = angle_tables(freq_index, token_index, length)
    inverse_real, inverse_imag = twist(
        inverse_real, inverse_imag, back_cos[:, :, None], back_sin[:, :, None], -1.0
    )
    pieces = lax.all_to_all(
        jnp.stack([inverse_real, inverse_imag]), "ctx", split_axis=2, concat_axis=1, tiled=True
    )
    real_rows = pieces[0].reshape(row_count, -1)
    imag_rows = pieces[1].reshape(row_count, -1)
    summed = jnp.dot(cos_rows.T, real_rows, precision=lax.Precision.HIGHEST) - jnp.dot(
        sin_rows.T, imag_rows, precision=lax.Precision.HIGHEST
    )
    columns = (summed * inverse_scale).reshape(groups, col_count, -1)
    gathered_rows = lax.all_to_all(columns, "ctx", split_axis=0, concat_axis=1, tiled=True)
    return gathered_rows.reshape(tokens_here, channels)


def local(query_branch, key_branch, value_branch, spectrum, skip_gain, out_weight):
    groups = lax.axis_size("ctx")
    position = lax.axis_index("ctx")
    mixed_in = (key_branch.astype(jnp.float32) * value_branch.astype(jnp.float32)).astype(
        jnp.bfloat16
    )
    convolved = sequence_path(mixed_in, spectrum, groups, position)
    gated_out = (
        query_branch.astype(jnp.float32) * (convolved + skip_gain * mixed_in.astype(jnp.float32))
    ).astype(jnp.bfloat16)
    summed = lax.psum_scatter(
        lax.dot_general(
            out_weight, gated_out, (((0,), (1,)), ((), ())), preferred_element_type=jnp.float32
        ).astype(jnp.bfloat16),
        "tp",
        scatter_dimension=0,
        tiled=True,
    ).astype(jnp.float32)
    return summed.T.astype(jnp.bfloat16)


def solution(mesh):
    placed = (
        P("ctx", "tp"),
        P("ctx", "tp"),
        P("ctx", "tp"),
        P(None, "ctx", None, "tp"),
        P("tp"),
        P("tp", None),
    )
    return jax.shard_map(
        local, mesh=mesh, in_specs=placed, out_specs=P("ctx", "tp"), check_vma=False
    )
```

profile of v0, /device:TPU:1, one launch (start us, length us, event | category | flops | bytes accessed | tf_op | source)
XLA Modules:
  0.0 229.8 jit_solution(951078676815630832)
XLA Ops:
  6.5 1.1 multiply_convert_fusion.1
  7.7 0.7 reshape.135
  8.4 21.7 %all-to-all-start = ((bf16[1,64,3,256]{3,2,0,1:T(4,128)(2,1)}), bf16[1,64,3,256]{3,2,0,1:T(4,128)(2,1)S(1)}, u32[]{:S(2)}, u32[]{:S(2)}) async-start(bf16[1,64,3,256]{3,2,0,1:T(4,128)(2,1)} %bitcast.1), calls=%async_computation | async-start | bytes 262144 | tf_op jit(solution)/shard_map/all_to_all | solution.py:50
  30.2 17.3 %all-to-all-done = bf16[1,64,3,256]{3,2,0,1:T(4,128)(2,1)S(1)} async-done(((bf16[1,64,3,256]{3,2,0,1:T(4,128)(2,1)}), bf16[1,64,3,256]{3,2,0,1:T(4,128)(2,1)S(1)}, u32[]{:S(2)}, u32[]{:S(2)}) %all-to-all-start) | async-done | bytes 98336 | tf_op jit(solution)/shard_map/all_to_all | solution.py:50
  47.5 0.5 convolution_negate_fusion
  48.0 0.6 add_bitcast_fusion.1
  48.6 1.5 copy.35
  50.1 5.3 %all-to-all-start.1 = ((f32[2,128,3,256]{3,0,2,1:T(2,128)}), f32[2,128,3,256]{3,0,2,1:T(2,128)S(1)}, u32[]{:S(2)}, u32[]{:S(2)}) async-start(f32[2,128,3,256]{3,0,2,1:T(2,128)} %copy.35), calls=%async_computation.1 | async-start | bytes 1572864 | tf_op jit(solution)/shard_map/all_to_all | solution.py:70
  55.8 26.2 %all-to-all-done.1 = f32[2,128,3,256]{3,0,2,1:T(2,128)S(1)} async-done(((f32[2,128,3,256]{3,0,2,1:T(2,128)}), f32[2,128,3,256]{3,0,2,1:T(2,128)S(1)}, u32[]{:S(2)}, u32[]{:S(2)}) %all-to-all-start.1) | async-done | bytes 786464 | tf_op jit(solution)/shard_map/all_to_all | solution.py:70
  82.7 1.3 fusion.6
  84.0 1.3 fusion.10
  85.2 1.3 fusion.1
  86.5 1.4 fusion.5
  87.9 1.3 fusion.18
  89.2 1.3 fusion.20
  90.5 1.3 convolution_add_fusion
  91.7 1.4 add_bitcast_fusion
  93.2 0.6 copy.41
  93.8 28.1 %all_to_all.48 = f32[2,2,192,256]{3,1,0,2:T(2,128)S(1)} all-to-all(f32[2,2,192,256]{3,1,0,2:T(2,128)S(1)} %copy.41), channel_id=1, replica_groups=mesh['ctx'=64,'tp'=8] {'ctx'}, dimensions={2} | all-to-all | bytes 1572864 | tf_op jit(solution)/shard_map/all_to_all | solution.py:80
  122.9 0.5 fusion.77
  123.4 0.5 fusion.3
  124.0 30.7 %all_to_all.49 = f32[64,3,256]{2,1,0:T(4,128)S(1)} all-to-all(f32[64,3,256]{2,1,0:T(4,128)S(1)} %reshape.137), channel_id=1, replica_groups=mesh['ctx'=64,'tp'=8] {'ctx'}, dimensions={0} | all-to-all | bytes 393216 | tf_op jit(solution)/shard_map/all_to_all | solution.py:89
  154.8 1.8 fusion
  156.6 66.3 %reduce-scatter.2.cloned.1.call-done = bf16[512,192]{0,1:T(8,128)(2,1)} async-done(((bf16[4096,192]{0,1:T(8,128)(2,1)}), bf16[512,192]{0,1:T(8,128)(2,1)}) %reduce-scatter.2.cloned.1.call-update) | async-done | bytes 196624 | tf_op jit(solution)/shard_map/reduce_scatter | solution.py:103
  (26 shorter events, 2.5 us)
Async XLA Ops:
  6.5 148.3 %copy-start = (bf16[256,4096]{1,0:T(8,128)(2,1)S(1)}, bf16[256,4096]{1,0:T(8,128)(2,1)}, u32[]{:S(2)}) copy-start(bf16[256,4096]{1,0:T(8,128)(2,1)} %param.11) | copy-start | bytes 6291460
  8.4 39.1 %all-to-all-start = ((bf16[1,64,3,256]{3,2,0,1:T(4,128)(2,1)}), bf16[1,64,3,256]{3,2,0,1:T(4,128)(2,1)S(1)}, u32[]{:S(2)}, u32[]{:S(2)}) async-start(bf16[1,64,3,256]{3,2,0,1:T(4,128)(2,1)} %bitcast.1), calls=%async_computation | async-start | bytes 262144 | tf_op jit(solution)/shard_map/all_to_all | solution.py:50
  50.1 31.8 %all-to-all-start.1 = ((f32[2,128,3,256]{3,0,2,1:T(2,128)}), f32[2,128,3,256]{3,0,2,1:T(2,128)S(1)}, u32[]{:S(2)}, u32[]{:S(2)}) async-start(f32[2,128,3,256]{3,0,2,1:T(2,128)} %copy.35), calls=%async_computation.1 | async-start | bytes 1572864 | tf_op jit(solution)/shard_map/all_to_all | solution.py:70
  55.4 167.5 %reduce-scatter.2.cloned.1.call-start = ((), (), s32[]{:S(2)}) async-start(), calls=%async_computation.5 | async-start | bytes 1769472 | tf_op jit(solution)/shard_map/reduce_scatter | solution.py:103
  82.4 4.1 %copy-start.1 = (f32[2,2,192,256]{3,2,1,0:T(8,128)S(1)}, f32[2,2,192,256]{3,2,1,0:T(8,128)}, u32[]{:S(2)}) copy-start(f32[2,2,192,256]{3,2,1,0:T(8,128)} %param.9) | copy-start | bytes 2359300
  122.8 32.0 %copy-start.2 = (bf16[192,256]{1,0:T(8,128)(2,1)S(1)}, bf16[192,256]{1,0:T(8,128)(2,1)}, u32[]{:S(2)}) copy-start(bf16[192,256]{1,0:T(8,128)(2,1)} %param.6) | copy-start | bytes 294916
  122.8 32.0 %copy-start.3 = (f32[256]{0:T(256)S(1)}, f32[256]{0:T(256)}, u32[]{:S(2)}) copy-start(f32[256]{0:T(256)} %param.10) | copy-start | bytes 3076
Sparse Core Ops, SparseCore 0:
  156.7 66.1 reduce-scatter.1
where the time goes:
time: 232 us; the launch traced here: 230 us
  waiting for transfers between devices  110 us (47%)
  blocking collectives  58.7 us (25%)
  starting transfers between devices  27.2 us (12%)
  matrix products  14.2 us (6%)
  between operations  13.7 us (6%)
  local copies, waits for them, and re-layouts  4.7 us (2%)
    reduce_scatter x1, waiting for transfers between devices, local(): lax.psum_scatter(lax.dot_general(out_weight, gated_out, (((0,), (1,)), ((...  66.3 us
    all_to_all x1, blocking collectives, sequence_path(): lax.all_to_all(columns, 'ctx', split_axis=0, concat_axis=1, tiled=True)  30.7 us
    all_to_all x1, blocking collectives, sequence_path(): lax.all_to_all(jnp.stack([inverse_real, inverse_imag]), 'ctx', split_axis...  28.1 us
    all_to_all x1, waiting for transfers between devices, sequence_path(): lax.all_to_all(spread, 'ctx', split_axis=1, concat_axis=2, tiled=True)  26.2 us
    all_to_all x1, starting transfers between devices, sequence_path(): lax.all_to_all(mixed_in.reshape(1, groups, col_count, channels), 'ctx', s...  21.7 us
    all_to_all x1, waiting for transfers between devices, sequence_path(): lax.all_to_all(mixed_in.reshape(1, groups, col_count, channels), 'ctx', s...  17.3 us
    dot_general x8, matrix products, transform_middle(): jnp.einsum('ka,rac->rkc', table, values, precision=lax.Precision.HIGHEST)  10.4 us
    all_to_all x1, starting transfers between devices, sequence_path(): lax.all_to_all(spread, 'ctx', split_axis=1, concat_axis=2, tiled=True)  5.29 us
  transfers between devices with their start and end apart: 3, of which 3 were waited for; matrix products, arithmetic and copies ran while one was open for 0% of the time, Pallas kernels for 0%

commit v1 on v0

v1 whole, which is shorter than its diff:
```python
import math

import jax
import jax.numpy as jnp
import numpy as np
from jax import lax
from jax.sharding import Mesh
from jax.sharding import PartitionSpec as P

CTX = ("x", "zh", "y")
TP = ("zl", "core")


def tables(groups, tokens):
    rows = 2 * groups
    local = rows // groups
    length = rows * tokens
    kb = (np.arange(local)[:, None] + local * np.arange(groups)[None, :]).reshape(-1)
    n1 = np.arange(groups)
    n2 = np.arange(tokens)
    first = 2.0 * math.pi * (np.outer(kb, n1) % rows) / rows
    middle = 2.0 * math.pi * (np.outer(n2, n2) % tokens) / tokens
    turn = 2.0 * math.pi * (np.outer(kb, n2) % length) / length
    fwd = np.concatenate([np.cos(first), -np.sin(first)], axis=0)
    back = np.concatenate([np.cos(first), -np.sin(first)], axis=0).T / length
    cos_m, sin_m = np.cos(middle), np.sin(middle)
    mid = np.block([[cos_m, -sin_m], [sin_m, cos_m]])
    return fwd, back, mid, np.cos(turn), np.sin(turn)


def bf(values):
    return jnp.asarray(values, jnp.bfloat16)


def dot(a, b, dims):
    return lax.dot_general(a, b, (dims, ((), ())), preferred_element_type=jnp.float32)


def convolve(signal, filt):
    groups, chans, tokens = signal.shape
    fwd, back, mid, tc, ts = tables(groups, tokens)
    rows = 2 * groups
    tc = jnp.asarray(tc, jnp.float32)[:, None, :]
    ts = jnp.asarray(ts, jnp.float32)[:, None, :]
    a = dot(bf(fwd), signal.reshape(groups, -1), ((1,), (0,)))
    a = a.reshape(2, rows, chans, tokens)
    are, aim = a[0] * tc + a[1] * ts, a[1] * tc - a[0] * ts
    a = jnp.concatenate([are, aim], axis=-1).astype(jnp.bfloat16)
    b = dot(a, bf(mid), ((2,), (0,)))
    bre, bim = b[..., :tokens], b[..., tokens:]
    h = filt.transpose(2, 3, 0, 1, 4).reshape(2, rows, chans, tokens).astype(jnp.float32)
    fre = bre * h[0] - bim * h[1]
    fim = bre * h[1] + bim * h[0]
    f = jnp.concatenate([fre, fim], axis=-1).astype(jnp.bfloat16)
    g = dot(f, bf(mid.T), ((2,), (0,)))
    gre, gim = g[..., :tokens], g[..., tokens:]
    hre, him = gre * tc - gim * ts, gim * tc + gre * ts
    g = jnp.stack([hre, him]).astype(jnp.bfloat16).reshape(2 * rows, chans * tokens)
    y = dot(bf(back), g, ((1,), (0,)))
    return y.astype(jnp.bfloat16).reshape(groups, chans, tokens)


def local(query_branch, key_branch, value_branch, spectrum, skip_gain, out_weight):
    groups = lax.axis_size(CTX)
    tokens, channels = query_branch.shape
    chans = channels // groups
    mixed = (key_branch.astype(jnp.float32) * value_branch.astype(jnp.float32)).astype(
        jnp.bfloat16
    )
    mixed_t = mixed.T
    filt_t = spectrum.astype(jnp.bfloat16).transpose(3, 0, 1, 2).reshape(channels, -1)
    payload = jnp.concatenate([mixed_t, filt_t], axis=1).reshape(groups, -1)
    got = lax.all_to_all(payload, CTX, 0, 0, tiled=True).reshape(groups, chans, -1)
    signal = got[:, :, :tokens]
    filt = got[:, :, tokens:].reshape(groups, chans, *spectrum.shape[:3])
    y = convolve(signal, filt)
    y = lax.all_to_all(y.reshape(groups, -1), CTX, 0, 0, tiled=True).reshape(channels, tokens)
    gated = (
        query_branch.T.astype(jnp.float32)
        * (y.astype(jnp.float32) + skip_gain[:, None] * mixed_t.astype(jnp.float32))
    ).astype(jnp.bfloat16)
    part = dot(out_weight, gated, ((0,), (0,))).astype(jnp.bfloat16)
    summed = lax.psum_scatter(part, TP, scatter_dimension=0, tiled=True)
    return summed.astype(jnp.float32).T.astype(jnp.bfloat16)


def solution(mesh):
    fine = Mesh(mesh.devices.reshape(4, 4, 4, 4, 2), ("x", "zh", "y", "zl", "core"))
    placed = (
        P(CTX, TP),
        P(CTX, TP),
        P(CTX, TP),
        P(None, CTX, None, TP),
        P(TP),
        P(TP, None),
    )
    return jax.shard_map(local, mesh=fine, in_specs=placed, out_specs=P(CTX, TP), check_vma=False)
```

time: 232 us -> 161 us (0.69)
  waiting for transfers between devices: 110 us -> 33.7 us
  starting transfers between devices: 27.2 us -> 0.01 us
  blocking collectives: 58.7 us -> 76 us
  other arithmetic: 1.48 us -> 15.2 us
  local copies, waits for them, and re-layouts: 4.7 us -> 16.2 us
  matrix products: 14.2 us -> 4.16 us
    all_to_all x2 -> x0, waiting for transfers between devices: 43.4 us -> none  [the longest x1 26.2 us: sequence_path(): lax.all_to_all(spread, 'ctx', split_axis=1, concat_axis=2, tiled=True)]
    reduce_scatter x1, waiting for transfers between devices: 66.3 us -> 33.7 us  [local(): summed = lax.psum_scatter(part, TP, scatter_dimension=0, tiled=True)]
    all_to_all x2 -> x0, starting transfers between devices: 27 us -> none  [the longest x1 21.7 us: sequence_path(): lax.all_to_all(mixed_in.reshape(1, groups, col_count, channels), 'ctx', s...]
    all_to_all x2, blocking collectives: 58.7 us -> 76 us  [the longest x1 45.9 us: local(): lax.all_to_all(payload, CTX, 0, 0, tiled=True).reshape(groups, chans, -1)]
    dot_general x13 -> x5, matrix products: 14.2 us -> 4.16 us  [dot(): lax.dot_general(a, b, (dims, ((), ())), preferred_element_type=jnp.float32)]
    all_to_all x0 -> x3, other arithmetic: none -> 8.59 us  [the longest x2 8.01 us: local(): lax.all_to_all(payload, CTX, 0, 0, tiled=True).reshape(groups, chans, -1)]
    slice x4 -> x8, local copies, waits for them, and re-layouts: 0.82 us -> 4.53 us  [the longest x3 2.12 us: convolve(): are, aim = (a[0] * tc + a[1] * ts, a[1] * tc - a[0] * ts)]
    unnamed x10 -> x28, local copies, waits for them, and re-layouts: 0.17 us -> 3.62 us
  transfers between devices with their start and end apart: 3 -> 1, of which waited for: 3 -> 1; matrix products, arithmetic and copies ran while one was open for 0% -> 0% of each run, Pallas kernels for 0% -> 0%
where the time goes in v1:
time: 161 us; the launch traced here: 159 us
  blocking collectives  76 us (47%)
  waiting for transfers between devices  33.7 us (21%)
  local copies, waits for them, and re-layouts  16.2 us (10%)
  other arithmetic  15.2 us (9%)
  between operations  13.7 us (9%)
  matrix products  4.16 us (3%)
    all_to_all x1, blocking collectives, local(): lax.all_to_all(payload, CTX, 0, 0, tiled=True).reshape(groups, chans, -1)  45.9 us
    reduce_scatter x1, waiting for transfers between devices, local(): summed = lax.psum_scatter(part, TP, scatter_dimension=0, tiled=True)  33.7 us
    all_to_all x1, blocking collectives, local(): lax.all_to_all(y.reshape(groups, -1), CTX, 0, 0, tiled=True)  30.1 us
    all_to_all x2, other arithmetic, local(): lax.all_to_all(payload, CTX, 0, 0, tiled=True).reshape(groups, chans, -1)  8.01 us
    dot_general x5, matrix products, dot(): lax.dot_general(a, b, (dims, ((), ())), preferred_element_type=jnp.float32)  4.16 us
    unnamed x28, local copies, waits for them, and re-layouts  3.62 us
  transfers between devices with their start and end apart: 1, of which 1 were waited for; matrix products, arithmetic and copies ran while one was open for 0% of the time, Pallas kernels for 0%

profile of v1, /device:TPU:1, one launch (start us, length us, event | category | flops | bytes accessed | tf_op | source)
XLA Modules:
  0.0 159.1 jit_solution(12531030104566446451)
XLA Ops:
  6.5 1.1 fusion.15
  7.8 1.2 convert_element_type.69
  9.1 1.0 pad_maximum_fusion
  10.2 2.3 %all_to_all.16 = bf16[64,1,3840]{2,1,0:T(2,128)(2,1)S(1)} reshape(bf16[256,960]{1,0:T(8,128)(2,1)} %pad_maximum_fusion) | data formatting | bytes 983040 | tf_op jit(solution)/shard_map/all_to_all | solution.py:73
  12.5 0.5 broadcast.5
  13.0 4.3 %reduce.3 = bf16[64,3840]{1,0:T(8,128)(2,1)} reduce(bf16[64,1,3840]{2,1,0:T(2,128)(2,1)S(1)} %all_to_all.16, bf16[]{:T(256)} %broadcast.5), dimensions={1}, to_apply=%all_to_all.16.reduce_sub_computation | reduce | bytes 983042 | tf_op jit(solution)/shard_map/all_to_all | solution.py:73
  17.3 1.2 reshape.49
  18.4 45.9 %all_to_all.19 = bf16[64,2,1920]{2,1,0:T(2,128)(2,1)} all-to-all(bf16[64,2,1920]{2,1,0:T(2,128)(2,1)S(1)} %reshape.49), channel_id=1, replica_groups=mesh['x'=4,'zh'=4,'y'=4,'zl'=4,'core'=2] {'x','zh','y'}, dimensions={0} | all-to-all | bytes 983040 | tf_op jit(solution)/shard_map/all_to_all | solution.py:73
  64.3 2.1 %reshape.50 = bf16[64,1,3840]{2,1,0:T(2,128)(2,1)S(1)} reshape(bf16[64,2,1920]{2,1,0:T(2,128)(2,1)} %all_to_all.19) | data formatting | bytes 983040
  66.5 3.7 %reduce = bf16[64,3840]{1,0:T(8,128)(2,1)} reduce(bf16[64,1,3840]{2,1,0:T(2,128)(2,1)S(1)} %reshape.50, bf16[]{:T(256)} %constant.21), dimensions={1}, to_apply=%all_to_all.13.reduce_sub_computation | reduce | bytes 983042 | tf_op jit(solution)/shard_map/all_to_all | solution.py:73
  70.2 1.7 %reshape.41 = bf16[64,4,960]{2,1,0:T(4,128)(2,1)S(1)} reshape(bf16[64,3840]{1,0:T(8,128)(2,1)} %reduce) | data formatting | bytes 983040 | tf_op jit(solution)/shard_map/reshape | solution.py:73
  72.4 1.0 copy_convert_fusion
  73.4 2.1 %reshape.44 = f32[64,4,2,2,192]{4,3,2,0,1:T(2,128)S(1)} reshape(f32[64,4,768]{2,0,1:T(8,128)} %copy_convert_fusion) | data formatting | bytes 1572864 | tf_op jit(solution)/shard_map/convert_element_type | solution.py:51
  75.9 0.8 copy.59
  76.7 0.8 copy.58
  77.8 0.8 fusion.21
  79.0 1.2 copy.51
  80.4 1.2 add_convert_fusion.2
  81.6 1.5 fusion.4
  85.1 0.6 reduce.4
  85.7 30.1 %all_to_all.20 = bf16[64,2,384]{2,1,0:T(2,128)(2,1)S(1)} all-to-all(bf16[64,2,384]{2,1,0:T(2,128)(2,1)S(1)} %reshape.51), channel_id=1, replica_groups=mesh['x'=4,'zh'=4,'y'=4,'zl'=4,'core'=2] {'x','zh','y'}, dimensions={0} | all-to-all | bytes 196608 | tf_op jit(solution)/shard_map/all_to_all | solution.py:77
  116.0 0.5 convert_reduce_fusion
  116.8 1.7 %fusion = bf16[4096,192]{0,1:T(8,128)(2,1)} fusion(bf16[256,4096]{1,0:T(8,128)(2,1)S(1)} %copy-done, bf16[192,256]{1,0:T(8,128)(2,1)S(1)} %copy-done.8, f32[256,192]{0,1:T(8,128)S(1)} %copy.62, bf16[256,192]{0,1:T(8,128)(2,1)S(1)} %copy-done.4, f32[256]{0:T(256)S(1)} %copy-done.10), kind=kOutput, calls=%fused_computation.1 | convolution fusion | flops 403734528 | bytes 4064256 | tf_op jit(solution)/shard_map/dot_general | solution.py:36
  118.6 33.7 %reduce-scatter.2.cloned.1.call-done = bf16[512,192]{0,1:T(8,128)(2,1)} async-done(((bf16[4096,192]{0,1:T(8,128)(2,1)}), bf16[512,192]{0,1:T(8,128)(2,1)}) %reduce-scatter.2.cloned.1.call-update) | async-done | bytes 196624 | tf_op jit(solution)/shard_map/reduce_scatter | solution.py:83
  (46 shorter events, 4.3 us)
Async XLA Ops:
  6.5 110.2 %copy-start = (bf16[256,4096]{1,0:T(8,128)(2,1)S(1)}, bf16[256,4096]{1,0:T(8,128)(2,1)}, u32[]{:S(2)}) copy-start(bf16[256,4096]{1,0:T(8,128)(2,1)} %param.17) | copy-start | bytes 6291460
  6.5 145.7 %reduce-scatter.2.cloned.1.call-start = ((), (), s32[]{:S(2)}) async-start(), calls=%async_computation.3 | async-start | bytes 1769472 | tf_op jit(solution)/shard_map/reduce_scatter | solution.py:83
  7.7 1.3 copy-start.3
  75.5 2.1 %copy-start.9 = (bf16[256,64]{1,0:T(8,128)(2,1)S(1)}, bf16[256,64]{1,0:T(8,128)(2,1)}, u32[]{:S(2)}) copy-start(bf16[256,64]{1,0:T(8,128)(2,1)} %constant.14.clone) | copy-start | bytes 98308
  80.3 2.7 %copy-start.1 = (f32[1,2,64,4,192]{4,2,1,3,0:T(8,128)S(1)}, f32[1,2,64,4,192]{4,2,1,3,0:T(8,128)}, u32[]{:S(2)}) copy-start(f32[1,2,64,4,192]{4,2,1,3,0:T(8,128)} %copy.59) | copy-start | bytes 1179652
  80.3 2.7 %copy-start.2 = (f32[1,2,64,4,192]{4,2,1,3,0:T(8,128)S(1)}, f32[1,2,64,4,192]{4,2,1,3,0:T(8,128)}, u32[]{:S(2)}) copy-start(f32[1,2,64,4,192]{4,2,1,3,0:T(8,128)} %copy.58) | copy-start | bytes 1179652
  81.5 1.8 %copy-start.7 = (bf16[384,384,1]{1,0,2:T(8,128)(2,1)S(1)}, bf16[384,384,1]{1,0,2:T(8,128)(2,1)}, u32[]{:S(2)}) copy-start(bf16[384,384,1]{1,0,2:T(8,128)(2,1)} %constant.20) | copy-start | bytes 884740
  83.1 0.9 copy-start.5
  83.1 1.0 copy-start.6
  84.0 0.8 copy-start.11
  84.3 32.5 %copy-start.4 = (bf16[256,192]{0,1:T(8,128)(2,1)S(1)}, bf16[256,192]{0,1:T(8,128)(2,1)}, u32[]{:S(2)}) copy-start(bf16[256,192]{0,1:T(8,128)(2,1)} %copy-done.3) | copy-start | bytes 294916
  84.3 32.5 %copy-start.8 = (bf16[192,256]{1,0:T(8,128)(2,1)S(1)}, bf16[192,256]{1,0:T(8,128)(2,1)}, u32[]{:S(2)}) copy-start(bf16[192,256]{1,0:T(8,128)(2,1)} %param.12) | copy-start | bytes 294916
  84.3 32.5 %copy-start.10 = (f32[256]{0:T(256)S(1)}, f32[256]{0:T(256)}, u32[]{:S(2)}) copy-start(f32[256]{0:T(256)} %param.16) | copy-start | bytes 3076
Sparse Core Ops, SparseCore 0:
  118.7 33.5 reduce-scatter.1

commit v2 on v1

v2 whole, which is shorter than its diff:
```python
import math

import jax
import jax.numpy as jnp
import numpy as np
from jax import lax
from jax.experimental import pallas as pl
from jax.experimental.pallas import tpu as pltpu
from jax.sharding import Mesh
from jax.sharding import PartitionSpec as P

CTX = ("x", "zh", "y")
LANES = 128
BLOCK = 256
CHANS = 4
TOKENS = 192
F32, BF16 = jnp.float32, jnp.bfloat16


def tables(groups):
    rows, length = 2 * groups, 2 * groups * TOKENS
    kb = (np.arange(2)[:, None] + 2 * np.arange(groups)[None, :]).reshape(-1)
    n1, n2 = np.arange(groups), np.arange(TOKENS)
    first = 2.0 * math.pi * (np.outer(kb, n1) % rows) / rows
    middle = 2.0 * math.pi * (np.outer(n2, n2) % TOKENS) / TOKENS
    turn = 2.0 * math.pi * (np.outer(kb, n2) % length) / length
    fwd = np.concatenate([np.cos(first), -np.sin(first)], axis=0)
    back = fwd.T / length
    pad = ((0, 0), (0, BLOCK - TOKENS))
    cos_m, sin_m = (np.pad(f(middle), (pad[1], pad[1])) for f in (np.cos, np.sin))
    mid = np.block([[cos_m, -sin_m], [sin_m, cos_m]])
    turn = np.stack([np.pad(np.cos(turn), pad), np.pad(np.sin(turn), pad)])
    return (
        jnp.asarray(fwd, BF16),
        jnp.asarray(back, BF16),
        jnp.asarray(mid, BF16),
        jnp.asarray(turn, F32),
    )


def dot(a, b, dims=((1,), (0,))):
    return lax.dot_general(a, b, (dims, ((), ())), preferred_element_type=F32)


def low_half(shape):
    return lax.broadcasted_iota(jnp.int32, shape, 0) % 8 < 4


def pack_kernel(k_ref, v_ref, h_ref, out_ref):
    mixed = (k_ref[...].astype(F32) * v_ref[...].astype(F32)).astype(BF16).astype(F32)
    half, rest = LANES, TOKENS - LANES

    def column(j):
        if j == 0:
            rows = mixed[:half]
        elif j == 1:
            rows = jnp.concatenate([mixed[half:], h_ref[3, pl.ds(0, rest), :]], axis=0)
        elif j % 2 == 0:
            rows = h_ref[j // 2 - 1, pl.ds(0, half), :]
        else:
            last = h_ref[j // 2 - 1, pl.ds(half, rest), :]
            more = (
                h_ref[3, pl.ds(rest * (j // 2), rest), :] if j < 7 else jnp.zeros_like(last)
            )
            rows = jnp.concatenate([last, more], axis=0)
        return rows.T

    for j in range(4):
        a, b = column(j), column(j + 4)
        channels = a.shape[0]
        low = low_half(a.shape)
        even = jnp.where(low, a, pltpu.roll(b, 4, axis=0))
        odd = jnp.where(low, pltpu.roll(a, channels - 4, axis=0), b)
        both = jnp.stack(
            [even.reshape(channels // 8, 8, LANES), odd.reshape(channels // 8, 8, LANES)], axis=1
        )
        out_ref[:, :, pl.ds(j * LANES, LANES)] = both.reshape(channels // 4, 8, LANES).astype(BF16)


def conv_kernel(got_ref, fwd_ref, back_ref, mid_ref, turn_ref, out_ref, wide_ref, flat_ref):
    groups = got_ref.shape[0]
    rows = 2 * groups
    for j in range(4):
        tiles = got_ref[:, :, pl.ds(j * LANES, LANES)].astype(F32)
        wide_ref[j] = tiles.reshape(8 * groups, LANES)
    lower = lax.broadcasted_iota(jnp.int32, (groups, LANES), 1) < TOKENS - LANES
    signal, filt = [], []
    for c in range(CHANS):
        x, h0, h1, h2 = (
            jnp.concatenate(
                [
                    wide_ref[2 * (block % 2) + j, pl.ds(first + c, groups, stride=8), :]
                    for j in range(2)
                ],
                axis=1,
            )
            for block, first in ((0, 0), (1, 0), (2, CHANS), (3, CHANS))
        )
        shift = LANES - (TOKENS - LANES)
        h3 = jnp.concatenate(
            [
                jnp.where(lower, pltpu.roll(x[:, LANES:], shift, axis=1), h0[:, LANES:]),
                pltpu.roll(h1[:, LANES:], shift, axis=1),
            ],
            axis=1,
        )
        signal.append(x)
        filt.append((jnp.concatenate([h0, h1], axis=0), jnp.concatenate([h2, h3], axis=0)))
    a = dot(fwd_ref[...], jnp.concatenate(signal, axis=1).astype(BF16))
    tc, ts = turn_ref[0], turn_ref[1]
    turned = []
    for c in range(CHANS):
        re, im = a[:rows, c * BLOCK : (c + 1) * BLOCK], a[rows:, c * BLOCK : (c + 1) * BLOCK]
        turned.append(jnp.concatenate([re * tc + im * ts, im * tc - re * ts], axis=1).astype(BF16))
    b = dot(jnp.concatenate(turned, axis=0), mid_ref[...])
    product = []
    for c in range(CHANS):
        re, im = b[c * rows : (c + 1) * rows, :BLOCK], b[c * rows : (c + 1) * rows, BLOCK:]
        hr, hi = filt[c]
        product.append(jnp.concatenate([re * hr - im * hi, re * hi + im * hr], axis=1).astype(BF16))
    g = dot(jnp.concatenate(product, axis=0), mid_ref[...], ((1,), (1,)))
    turned = []
    for c in range(CHANS):
        re, im = g[c * rows : (c + 1) * rows, :BLOCK], g[c * rows : (c + 1) * rows, BLOCK:]
        turned.append(jnp.concatenate([re * tc - im * ts, im * tc + re * ts], axis=0).astype(BF16))
    y = dot(back_ref[...], jnp.concatenate(turned, axis=1))
    for c in range(CHANS):
        for half in range(2):
            start = c * BLOCK + half * LANES
            flat_ref[pl.ds(half * CHANS + c, groups, stride=8), :] = y[:, start : start + LANES]
    out_ref[...] = flat_ref[...].astype(BF16).reshape(out_ref.shape)


def gate_kernel(got_ref, q_ref, k_ref, v_ref, skip_ref, out_ref):
    groups = got_ref.shape[0]
    tiles = got_ref[...].astype(F32).reshape(groups // 2, 2, 8, LANES)
    even = tiles[:, 0].reshape(4 * groups, LANES)
    odd = tiles[:, 1].reshape(4 * groups, LANES)
    low = low_half(even.shape)
    first = jnp.where(low, even, pltpu.roll(odd, 4, axis=0))
    second = jnp.where(low, pltpu.roll(even, 4 * groups - 4, axis=0), odd)
    conv = jnp.concatenate([first.T, second.T[: TOKENS - LANES]], axis=0)
    mixed = (k_ref[...].astype(F32) * v_ref[...].astype(F32)).astype(BF16).astype(F32)
    gated = q_ref[...].astype(F32) * (conv + skip_ref[...] * mixed)
    out_ref[...] = gated.astype(BF16)


def call(kernel, shape, args, scratch=()):
    return pl.pallas_call(
        kernel,
        out_shape=jax.ShapeDtypeStruct(shape, BF16),
        scratch_shapes=list(scratch),
        compiler_params=pltpu.CompilerParams(vmem_limit_bytes=40 * 2**20),
    )(*args)


def local(query_branch, key_branch, value_branch, spectrum, skip_gain, out_weight):
    groups = lax.axis_size(CTX)
    tokens, channels = query_branch.shape
    lines, cores = lax.axis_size("zl"), lax.axis_size("core")
    width = out_weight.shape[1] // (lines * cores)
    core = lax.axis_index("core")
    by_core = out_weight.reshape(channels, lines, cores, width)
    mine = lax.dynamic_index_in_dim(by_core, core, 2, keepdims=False)
    other = lax.dynamic_index_in_dim(by_core, 1 - core, 2, keepdims=False)
    other = lax.ppermute(other, "core", [(0, 1), (1, 0)])
    payload = call(
        pack_kernel,
        (groups, 8, 4 * LANES),
        (key_branch, value_branch, spectrum.reshape(4, tokens, channels)),
    )
    got = lax.all_to_all(payload, CTX, 0, 0, tiled=True)
    y = call(
        conv_kernel,
        (groups, 8, LANES),
        (got, *tables(groups)),
        [pltpu.VMEM((4, 8 * groups, LANES), F32), pltpu.VMEM((8 * groups, LANES), F32)],
    )
    y = lax.all_to_all(y, CTX, 0, 0, tiled=True)
    gated = call(
        gate_kernel,
        (tokens, channels),
        (y, query_branch, key_branch, value_branch, skip_gain.reshape(1, channels)),
    )
    near = lax.all_gather(gated, "core", axis=0)
    ours = lax.dynamic_index_in_dim(near, core, 0, keepdims=False)
    theirs = lax.dynamic_index_in_dim(near, 1 - core, 0, keepdims=False)
    dims = ((1,), (0,))
    part = dot(ours, mine, dims) + dot(theirs, other, dims)
    part = part.astype(BF16).transpose(1, 0, 2)
    part = lax.all_to_all(part, "zl", 0, 0, tiled=True)
    return jnp.sum(part.astype(F32), axis=0).astype(BF16)


def solution(mesh):
    fine = Mesh(mesh.devices.reshape(4, 4, 4, 4, 2), ("x", "zh", "y", "zl", "core"))
    tp = ("zl", "core")
    placed = (
        P(CTX, tp),
        P(CTX, tp),
        P(CTX, tp),
        P(None, CTX, None, tp),
        P(tp),
        P(tp, None),
    )
    return jax.shard_map(local, mesh=fine, in_specs=placed, out_specs=P(CTX, tp), check_vma=False)
```

time: 161 us -> 115 us (0.71)
  starting transfers between devices: 0.01 us -> 24.6 us
  blocking collectives: 76 us -> 56.3 us
  waiting for transfers between devices: 33.7 us -> 15.3 us
  other arithmetic: 15.2 us -> 0.82 us
  between operations: 13.7 us -> 0.14 us
  local copies, waits for them, and re-layouts: 16.2 us -> 12.5 us
  Pallas kernels: 0 us -> 2.47 us
  matrix products: 4.16 us -> 2.4 us
    reduce_scatter x1 -> x0, waiting for transfers between devices: 33.7 us -> none  [local(): summed = lax.psum_scatter(part, TP, scatter_dimension=0, tiled=True)]
    all_to_all x2, blocking collectives: 76 us -> 49.9 us  [the longest x1 26.9 us: local(): y = lax.all_to_all(y, CTX, 0, 0, tiled=True)]
    all_to_all x0 -> x1, starting transfers between devices: none -> 21.7 us  [local(): got = lax.all_to_all(payload, CTX, 0, 0, tiled=True)]
    all_to_all x0 -> x1, waiting for transfers between devices: none -> 15.3 us  [local(): got = lax.all_to_all(payload, CTX, 0, 0, tiled=True)]
    all_to_all x3 -> x0, other arithmetic: 8.59 us -> none  [the longest x2 8.01 us: local(): lax.all_to_all(payload, CTX, 0, 0, tiled=True).reshape(groups, chans, -1)]
    all_gather x0 -> x1, blocking collectives: none -> 6.35 us  [local(): near = lax.all_gather(gated, 'core', axis=0)]
    dynamic_slice x0 -> x1, local copies, waits for them, and re-layouts: none -> 5.65 us  [local(): other = lax.dynamic_index_in_dim(by_core, 1 - core, 2, keepdims=False)]
    slice x8 -> x0, local copies, waits for them, and re-layouts: 4.53 us -> none  [the longest x3 2.12 us: convolve(): are, aim = (a[0] * tc + a[1] * ts, a[1] * tc - a[0] * ts)]
  transfers between devices with their start and end apart: 1 -> 2, of which waited for: 1 -> 1; matrix products, arithmetic and copies ran while one was open for 0% -> 9% of each run, Pallas kernels for 0% -> 1%
where the time goes in v2:
time: 115 us
  blocking collectives  56.3 us (49%)
  starting transfers between devices  24.6 us (21%)
  waiting for transfers between devices  15.3 us (13%)
  local copies, waits for them, and re-layouts  12.5 us (11%)
  Pallas kernels  2.47 us (2%)
  matrix products  2.4 us (2%)
    all_to_all x1, blocking collectives, local(): y = lax.all_to_all(y, CTX, 0, 0, tiled=True)  26.9 us
    all_to_all x1, blocking collectives, local(): part = lax.all_to_all(part, 'zl', 0, 0, tiled=True)  23 us
    all_to_all x1, starting transfers between devices, local(): got = lax.all_to_all(payload, CTX, 0, 0, tiled=True)  21.7 us
    all_to_all x1, waiting for transfers between devices, local(): got = lax.all_to_all(payload, CTX, 0, 0, tiled=True)  15.3 us
    all_gather x1, blocking collectives, local(): near = lax.all_gather(gated, 'core', axis=0)  6.35 us
    dynamic_slice x1, local copies, waits for them, and re-layouts, local(): other = lax.dynamic_index_in_dim(by_core, 1 - core, 2, keepdims=False)  5.65 us
    unnamed x25, local copies, waits for them, and re-layouts  3.54 us
    reshape x1, local copies, waits for them, and re-layouts, local(): by_core = out_weight.reshape(channels, lines, cores, width)  3.3 us
  transfers between devices with their start and end apart: 2, of which 1 were waited for; matrix products, arithmetic and copies ran while one was open for 9% of the time, Pallas kernels for 1%

profile of v2, /device:TPU:1, one launch (start us, length us, event | category | flops | bytes accessed | tf_op | source)
XLA Modules:
  0.0 114.5 jit_solution(1704578043406458587)
XLA Ops:
  0.0 1.1 copy-done
  1.1 0.9 copy-done.2
  2.0 0.9 copy-done.4
  2.9 1.1 shard_map.100
  4.0 21.7 %all-to-all-start = ((bf16[64,8,512]{2,1,0:T(8,128)(2,1)}), bf16[64,8,512]{2,1,0:T(8,128)(2,1)S(1)}, u32[]{:S(2)}, u32[]{:S(2)}) async-start(bf16[64,8,512]{2,1,0:T(8,128)(2,1)} %shard_map.100), calls=%async_computation | async-start | bytes 1048576 | tf_op jit(solution)/shard_map/all_to_all | solution.py:172
  25.8 3.3 %reshape.11 = bf16[256,4,2,512]{3,2,1,0:T(2,128)(2,1)S(1)} reshape(bf16[256,4096]{1,0:T(8,128)(2,1)} %param.15) | data formatting | bytes 4194304 | tf_op jit(solution)/shard_map/reshape | solution.py:163
  29.1 5.6 %constant_dynamic-slice_fusion = (bf16[256,4,1,512]{3,2,1,0:T(2,128)(2,1)S(1)}, bf16[256,4,1,512]{3,2,1,0:T(2,128)(2,1)}) fusion(bf16[256,4,2,512]{3,2,1,0:T(2,128)(2,1)S(1)} %reshape.11, s32[]{:T(128)S(6)} %select_n.11, s32[]{:T(128)S(6)} %select_n.10), kind=kLoop, calls=%fused_computation.9 | loop fusion | bytes 4194312 | tf_op jit(solution)/shard_map/jit(dynamic_index_in_dim)/dynamic_slice | solution.py:165
  34.7 0.0 copy-start.3
  34.8 0.0 copy-start.5
  34.8 0.0 copy-start.7
  34.8 0.0 copy-start.10
  34.8 0.6 copy.18
  35.4 2.9 %collective-permute-start = (bf16[256,4,512]{2,0,1:T(8,128)(2,1)S(1)}, bf16[256,4,512]{2,0,1:T(8,128)(2,1)}, u32[]{:S(2)}, u32[]{:S(2)}) collective-permute-start(bf16[256,4,512]{2,0,1:T(8,128)(2,1)S(1)} %bitcast.22), channel_id=1, source_target_pairs={{0,1},{1,0},{2,3},{3,2},{4,5},{5,4},{6,7},{7,6},{8,9},{9,8},{10,11... | collective-permute-start | bytes 3145736 | tf_op jit(solution)/shard_map/ppermute | solution.py:166
  38.2 15.3 %all-to-all-done.got_ref = bf16[64,8,512]{2,1,0:T(8,128)(2,1)S(1)} async-done(((bf16[64,8,512]{2,1,0:T(8,128)(2,1)}), bf16[64,8,512]{2,1,0:T(8,128)(2,1)S(1)}, u32[]{:S(2)}, u32[]{:S(2)}) %all-to-all-start) | async-done | bytes 524320 | tf_op jit(solution)/shard_map/all_to_all | solution.py:172
  53.5 0.0 copy-done.1
  53.6 1.2 %shard_map.101 = bf16[64,8,128]{2,1,0:T(8,128)(2,1)S(1)} custom-call(bf16[64,8,512]{2,1,0:T(8,128)(2,1)S(1)} %all-to-all-done.got_ref, bf16[256,64]{1,0:T(8,128)(2,1)S(1)} %copy-done.8, bf16[64,256]{1,0:T(8,128)(2,1)S(1)} %copy-done.9, bf16[512,512]{1,0:T(8,128)(2,1)S(1)} %copy-done.1, f32[2,128,256]{2,1,0:T(8,128)S(1)} %copy-done.6), custom_call_target="tpu_custom_call" | custom-call | tf_op jit(solution)/shard_map/pallas_call | solution.py:149
  54.8 26.9 %all_to_all.15.got_ref = bf16[64,8,128]{2,1,0:T(8,128)(2,1)S(1)} all-to-all(bf16[64,8,128]{2,1,0:T(8,128)(2,1)S(1)} %shard_map.101), channel_id=1, replica_groups=mesh['x'=4,'zh'=4,'y'=4,'zl'=4,'core'=2] {'x','zh','y'}, dimensions={0} | all-to-all | bytes 262144 | tf_op jit(solution)/shard_map/all_to_all | solution.py:179
  81.7 0.1 shard_map.102
  81.9 6.4 %all-gather = bf16[384,256]{1,0:T(8,128)(2,1)S(1)} all-gather(bf16[192,256]{1,0:T(8,128)(2,1)S(1)} %shard_map.102), channel_id=2, replica_groups=mesh['x'=4,'zh'=4,'y'=4,'zl'=4,'core'=2] {'core'}, dimensions={0}, use_global_device_ids=true | all-gather | bytes 294912 | tf_op jit(solution)/shard_map/all_gather | solution.py:185
  88.2 0.8 fusion.1
  89.0 0.0 collective-permute-done
  89.0 1.6 %fusion = bf16[4,192,512]{2,1,0:T(8,128)(2,1)S(1)} fusion(f32[192,4,512]{2,0,1:T(8,128)S(1)} %fusion.1, bf16[256,4,512]{2,0,1:T(8,128)(2,1)} %collective-permute-done, bf16[2,192,256]{2,1,0:T(8,128)(2,1)S(1)} %bitcast.24, s32[]{:T(128)S(6)} %select_n.11), kind=kOutput, calls=%fused_computation.1 | convolution fusion | flops 202113024 | bytes 3506180 | tf_op jit(solution)/shard_map/dot_general | solution.py:42
  90.7 23.0 %all_to_all.16 = bf16[4,192,512]{2,1,0:T(8,128)(2,1)S(1)} all-to-all(bf16[4,192,512]{2,1,0:T(8,128)(2,1)S(1)} %fusion), channel_id=1, replica_groups=mesh['x'=4,'zh'=4,'y'=4,'zl'=4,'core'=2] {'zl'}, dimensions={0} | all-to-all | bytes 1572864 | tf_op jit(solution)/shard_map/all_to_all | solution.py:191
  113.7 0.8 reduce_sum.12
  (16 shorter events, 0.0 us)
Async XLA Ops:
  0.0 1.1 copy-start
  1.1 0.9 copy-start.2
  2.0 0.9 copy-start.4
  4.0 49.5 %all-to-all-start = ((bf16[64,8,512]{2,1,0:T(8,128)(2,1)}), bf16[64,8,512]{2,1,0:T(8,128)(2,1)S(1)}, u32[]{:S(2)}, u32[]{:S(2)}) async-start(bf16[64,8,512]{2,1,0:T(8,128)(2,1)} %shard_map.100), calls=%async_computation | async-start | bytes 1048576 | tf_op jit(solution)/shard_map/all_to_all | solution.py:172
  34.7 18.8 %copy-start.1 = (bf16[512,512]{1,0:T(8,128)(2,1)S(1)}, bf16[512,512]{1,0:T(8,128)(2,1)}, u32[]{:S(2)}) copy-start(bf16[512,512]{1,0:T(8,128)(2,1)} %constant.35.clone.mid_ref) | copy-start | bytes 1572868
  34.7 18.8 %copy-start.6 = (f32[2,128,256]{2,1,0:T(8,128)S(1)}, f32[2,128,256]{2,1,0:T(8,128)}, u32[]{:S(2)}) copy-start(f32[2,128,256]{2,1,0:T(8,128)} %constant.36.clone.turn_ref) | copy-start | bytes 786436
  34.7 18.8 %copy-start.8 = (bf16[256,64]{1,0:T(8,128)(2,1)S(1)}, bf16[256,64]{1,0:T(8,128)(2,1)}, u32[]{:S(2)}) copy-start(bf16[256,64]{1,0:T(8,128)(2,1)} %constant.33.clone.fwd_ref) | copy-start | bytes 98308
  34.7 18.8 %copy-start.9 = (bf16[64,256]{1,0:T(8,128)(2,1)S(1)}, bf16[64,256]{1,0:T(8,128)(2,1)}, u32[]{:S(2)}) copy-start(bf16[64,256]{1,0:T(8,128)(2,1)} %constant.34.clone.back_ref) | copy-start | bytes 98308
  34.7 47.0 %copy-start.3 = (bf16[192,256]{1,0:T(8,128)(2,1)S(1)}, bf16[192,256]{1,0:T(8,128)(2,1)}, u32[]{:S(2)}) copy-start(bf16[192,256]{1,0:T(8,128)(2,1)} %k_ref.3) | copy-start | bytes 294916
  34.8 47.0 %copy-start.5 = (bf16[192,256]{1,0:T(8,128)(2,1)S(1)}, bf16[192,256]{1,0:T(8,128)(2,1)}, u32[]{:S(2)}) copy-start(bf16[192,256]{1,0:T(8,128)(2,1)} %v_ref.3) | copy-start | bytes 294916
  34.8 47.0 %copy-start.7 = (bf16[192,256]{1,0:T(8,128)(2,1)S(1)}, bf16[192,256]{1,0:T(8,128)(2,1)}, u32[]{:S(2)}) copy-start(bf16[192,256]{1,0:T(8,128)(2,1)} %q_ref.1) | copy-start | bytes 294916
  34.8 47.0 %copy-start.10 = (f32[256]{0:T(256)S(1)}, f32[256]{0:T(256)}, u32[]{:S(2)}) copy-start(f32[256]{0:T(256)} %param.14) | copy-start | bytes 3076
  35.4 53.7 %collective-permute-start = (bf16[256,4,512]{2,0,1:T(8,128)(2,1)S(1)}, bf16[256,4,512]{2,0,1:T(8,128)(2,1)}, u32[]{:S(2)}, u32[]{:S(2)}) collective-permute-start(bf16[256,4,512]{2,0,1:T(8,128)(2,1)S(1)} %bitcast.22), channel_id=1, source_target_pairs={{0,1},{1,0},{2,3},{3,2},{4,5},{5,4},{6,7},{7,6},{8,9},{9,8},{10,11... | collective-permute-start | bytes 3145736 | tf_op jit(solution)/shard_map/ppermute | solution.py:166
  53.6 34.7 %copy-start.11 = (bf16[256,4,1,512]{3,2,1,0:T(2,128)(2,1)S(1)}, bf16[256,4,1,512]{3,2,1,0:T(2,128)(2,1)}, u32[]{:S(2)}) copy-start(bf16[256,4,1,512]{3,2,1,0:T(2,128)(2,1)} %get-tuple-element.6) | copy-start | bytes 3145732

commit v3 on v2

--- a/solution.py
+++ b/solution.py
@@ -46,7 +46,13 @@
     return lax.broadcasted_iota(jnp.int32, shape, 0) % 8 < 4
 
 
-def pack_kernel(k_ref, v_ref, h_ref, out_ref):
+def pack_kernel(k_hbm, v_hbm, h_hbm, out_ref, k_ref, v_ref, h_ref, sems):
+    pairs = ((k_hbm, k_ref), (v_hbm, v_ref), (h_hbm, h_ref))
+    copies = [pltpu.make_async_copy(a, b, sems.at[i]) for i, (a, b) in enumerate(pairs)]
+    for copy in copies:
+        copy.start()
+    for copy in copies:
+        copy.wait()
     mixed = (k_ref[...].astype(F32) * v_ref[...].astype(F32)).astype(BF16).astype(F32)
     half, rest = LANES, TOKENS - LANES
 
@@ -145,13 +151,49 @@
     out_ref[...] = gated.astype(BF16)
 
 
-def call(kernel, shape, args, scratch=()):
-    return pl.pallas_call(
+def split_kernel(w_hbm, mine_hbm, other_hbm, sems):
+    core = lax.axis_index("core")
+    lines, _, width = mine_hbm.shape
+    copies = []
+    for line in range(lines):
+        for side, (out, owner) in enumerate(((mine_hbm, core), (other_hbm, 1 - core))):
+            start = pl.multiple_of((2 * line + owner) * width, LANES)
+            copies.append(
+                pltpu.make_async_copy(
+                    w_hbm.at[:, pl.ds(start, width)], out.at[line], sems.at[2 * line + side]
+                )
+            )
+    for copy in copies:
+        copy.start()
+    for copy in copies:
+        copy.wait()
+
+
+def project_kernel(near_ref, mine_ref, other_ref, *outs):
+    core, line = lax.axis_index("core"), lax.axis_index("zl")
+    ours, theirs = near_ref[core], near_ref[1 - core]
+    for d, out in enumerate(outs):
+        dest = line ^ d
+        out[...] = (dot(ours, mine_ref[dest]) + dot(theirs, other_ref[dest])).astype(BF16)
+
+
+def call(kernel, shapes, args, scratch=(), hbm=False, hbm_out=False):
+    many = isinstance(shapes, list)
+    out_shape = [jax.ShapeDtypeStruct(s, BF16) for s in (shapes if many else [shapes])]
+    extra = {}
+    if not hbm:
+        extra["compiler_params"] = pltpu.CompilerParams(vmem_limit_bytes=24 * 2**20)
+    else:
+        extra["in_specs"] = [pl.BlockSpec(memory_space=pltpu.HBM)] * len(args)
+    if hbm_out:
+        extra["out_specs"] = [pl.BlockSpec(memory_space=pl.ANY)] * len(out_shape)
+    out = pl.pallas_call(
         kernel,
-        out_shape=jax.ShapeDtypeStruct(shape, BF16),
+        out_shape=out_shape,
         scratch_shapes=list(scratch),
-        compiler_params=pltpu.CompilerParams(vmem_limit_bytes=40 * 2**20),
+        **extra,
     )(*args)
+    return out if many else out[0]
 
 
 def local(query_branch, key_branch, value_branch, spectrum, skip_gain, out_weight):
@@ -159,17 +201,28 @@
     tokens, channels = query_branch.shape
     lines, cores = lax.axis_size("zl"), lax.axis_size("core")
     width = out_weight.shape[1] // (lines * cores)
-    core = lax.axis_index("core")
-    by_core = out_weight.reshape(channels, lines, cores, width)
-    mine = lax.dynamic_index_in_dim(by_core, core, 2, keepdims=False)
-    other = lax.dynamic_index_in_dim(by_core, 1 - core, 2, keepdims=False)
-    other = lax.ppermute(other, "core", [(0, 1), (1, 0)])
     payload = call(
         pack_kernel,
         (groups, 8, 4 * LANES),
         (key_branch, value_branch, spectrum.reshape(4, tokens, channels)),
+        [
+            pltpu.VMEM((tokens, channels), BF16),
+            pltpu.VMEM((tokens, channels), BF16),
+            pltpu.VMEM((4, tokens, channels), F32),
+            pltpu.SemaphoreType.DMA((3,)),
+        ],
+        hbm=True,
     )
     got = lax.all_to_all(payload, CTX, 0, 0, tiled=True)
+    mine, other = call(
+        split_kernel,
+        [(lines, channels, width)] * 2,
+        (out_weight,),
+        [pltpu.SemaphoreType.DMA((2 * lines,))],
+        hbm=True,
+        hbm_out=True,
+    )
+    other = lax.ppermute(other, "core", [(0, 1), (1, 0)])
     y = call(
         conv_kernel,
         (groups, 8, LANES),
@@ -183,13 +236,12 @@
         (y, query_branch, key_branch, value_branch, skip_gain.reshape(1, channels)),
     )
     near = lax.all_gather(gated, "core", axis=0)
-    ours = lax.dynamic_index_in_dim(near, core, 0, keepdims=False)
-    theirs = lax.dynamic_index_in_dim(near, 1 - core, 0, keepdims=False)
-    dims = ((1,), (0,))
-    part = dot(ours, mine, dims) + dot(theirs, other, dims)
-    part = part.astype(BF16).transpose(1, 0, 2)
-    part = lax.all_to_all(part, "zl", 0, 0, tiled=True)
-    return jnp.sum(part.astype(F32), axis=0).astype(BF16)
+    pieces = call(project_kernel, [(tokens, width)] * lines, (near, mine, other))
+    total = pieces[0].astype(F32)
+    for d in (3, 2, 1):
+        back = lax.ppermute(pieces[d], "zl", [(i, i ^ d) for i in range(lines)])
+        total = total + back.astype(F32)
+    return total.astype(BF16)
 
 
 def solution(mesh):

time: 115 us -> 157 us (1.37)
  Pallas kernels: 2.47 us -> 69 us
  blocking collectives: 56.3 us -> 38.2 us
  local copies, waits for them, and re-layouts: 12.5 us -> 0.99 us
  starting transfers between devices: 24.6 us -> 34 us
  matrix products: 2.4 us -> 0 us
    pallas_call x3 -> x5, Pallas kernels: 2.47 us -> 69 us  [call(): pl.pallas_call(kernel, out_shape=out_shape, scratch_shapes=list(scratch),...]
    all_to_all x1 -> x0, blocking collectives: 23 us -> none  [local(): part = lax.all_to_all(part, 'zl', 0, 0, tiled=True)]
    all_to_all x1, waiting for transfers between devices: 15.3 us -> 0.01 us  [local(): got = lax.all_to_all(payload, CTX, 0, 0, tiled=True)]
    ppermute x0 -> x3, waiting for transfers between devices: none -> 13.9 us  [local(): back = lax.ppermute(pieces[d], 'zl', [(i, i ^ d) for i in range(lines)])]
    ppermute x0 -> x3, starting transfers between devices: none -> 9.27 us  [local(): back = lax.ppermute(pieces[d], 'zl', [(i, i ^ d) for i in range(lines)])]
    all_to_all x1, blocking collectives: 26.9 us -> 34 us  [local(): y = lax.all_to_all(y, CTX, 0, 0, tiled=True)]
    dynamic_slice x1 -> x0, local copies, waits for them, and re-layouts: 5.65 us -> none  [local(): other = lax.dynamic_index_in_dim(by_core, 1 - core, 2, keepdims=False)]
    reshape x1 -> x0, local copies, waits for them, and re-layouts: 3.3 us -> none  [local(): by_core = out_weight.reshape(channels, lines, cores, width)]
  transfers between devices with their start and end apart: 2 -> 5, of which waited for: 1 -> 2; matrix products, arithmetic and copies ran while one was open for 9% -> 0% of each run, Pallas kernels for 1% -> 42%
where the time goes in v3:
time: 157 us
  Pallas kernels  69 us (44%)
  blocking collectives  38.2 us (24%)
  starting transfers between devices  34 us (22%)
  waiting for transfers between devices  13.9 us (9%)
    pallas_call x5, Pallas kernels, call(): pl.pallas_call(kernel, out_shape=out_shape, scratch_shapes=list(scratch),...  69 us
    all_to_all x1, blocking collectives, local(): y = lax.all_to_all(y, CTX, 0, 0, tiled=True)  34 us
    all_to_all x1, starting transfers between devices, local(): got = lax.all_to_all(payload, CTX, 0, 0, tiled=True)  21.8 us
    ppermute x3, waiting for transfers between devices, local(): back = lax.ppermute(pieces[d], 'zl', [(i, i ^ d) for i in range(lines)])  13.9 us
    ppermute x3, starting transfers between devices, local(): back = lax.ppermute(pieces[d], 'zl', [(i, i ^ d) for i in range(lines)])  9.27 us
    all_gather x1, blocking collectives, local(): near = lax.all_gather(gated, 'core', axis=0)  4.25 us
  transfers between devices with their start and end apart: 5, of which 2 were waited for; matrix products, arithmetic and copies ran while one was open for 0% of the time, Pallas kernels for 42%

profile of v3, /device:TPU:1, one launch (start us, length us, event | category | flops | bytes accessed | tf_op | source)
XLA Modules:
  0.0 157.1 jit_solution(5371721908489377167)
XLA Ops:
  0.0 2.4 %shard_map.100 = bf16[64,8,512]{2,1,0:T(8,128)(2,1)} custom-call(bf16[192,256]{1,0:T(8,128)(2,1)} %k_ref.1, bf16[192,256]{1,0:T(8,128)(2,1)} %v_ref.1, f32[4,192,256]{2,1,0:T(8,128)} %bitcast.5), custom_call_target="tpu_custom_call" | custom-call | tf_op jit(solution)/shard_map/pallas_call | solution.py:190
  2.4 21.8 %all-to-all-start = ((bf16[64,8,512]{2,1,0:T(8,128)(2,1)}), bf16[64,8,512]{2,1,0:T(8,128)(2,1)S(1)}, u32[]{:S(2)}, u32[]{:S(2)}) async-start(bf16[64,8,512]{2,1,0:T(8,128)(2,1)} %shard_map.100), calls=%async_computation | async-start | bytes 1048576 | tf_op jit(solution)/shard_map/all_to_all | solution.py:216
  24.2 0.0 copy-start.2
  24.2 0.0 copy-start.3
  24.2 0.0 copy-start.5
  24.2 0.0 copy-start.8
  24.2 64.7 %shard_map.103 = (bf16[4,256,512]{2,1,0:T(8,128)(2,1)}, bf16[4,256,512]{2,1,0:T(8,128)(2,1)}) custom-call(bf16[256,4096]{1,0:T(8,128)(2,1)} %w_hbm.1), custom_call_target="tpu_custom_call" | custom-call | tf_op jit(solution)/shard_map/pallas_call | solution.py:190
  89.0 3.0 %collective-permute-start = (bf16[4,256,512]{2,1,0:T(8,128)(2,1)}, bf16[4,256,512]{2,1,0:T(8,128)(2,1)S(1)}, u32[]{:S(2)}, u32[]{:S(2)}) collective-permute-start(bf16[4,256,512]{2,1,0:T(8,128)(2,1)} %get-tuple-element.12), channel_id=1, source_target_pairs={{0,1},{1,0},{2,3},{3,2},{4,5},{5,4},{6,7},{7,6},{8,9},{9,8},{10,11... | collective-permute-start | bytes 3145736 | tf_op jit(solution)/shard_map/ppermute | solution.py:225
  92.0 0.0 all-to-all-done.got_ref
  92.0 0.0 copy-start.4
  92.0 0.9 copy-done.4
  93.0 1.2 shard_map.101
  94.2 34.0 %all_to_all.10.got_ref = bf16[64,8,128]{2,1,0:T(8,128)(2,1)S(1)} all-to-all(bf16[64,8,128]{2,1,0:T(8,128)(2,1)S(1)} %shard_map.101), channel_id=1, replica_groups=mesh['x'=4,'zh'=4,'y'=4,'zl'=4,'core'=2] {'x','zh','y'}, dimensions={0} | all-to-all | bytes 262144 | tf_op jit(solution)/shard_map/all_to_all | solution.py:232
  128.2 0.1 shard_map.102
  128.3 4.2 %all-gather = bf16[384,256]{1,0:T(8,128)(2,1)S(1)} all-gather(bf16[192,256]{1,0:T(8,128)(2,1)S(1)} %shard_map.102), channel_id=2, replica_groups=mesh['x'=4,'zh'=4,'y'=4,'zl'=4,'core'=2] {'core'}, dimensions={0}, use_global_device_ids=true | all-gather | bytes 294912 | tf_op jit(solution)/shard_map/all_gather | solution.py:238
  132.5 0.0 collective-permute-done.other_ref
  132.5 0.6 shard_map.104
  133.1 3.5 %collective-permute-start.1 = (bf16[192,512]{1,0:T(8,128)(2,1)S(1)}, bf16[192,512]{1,0:T(8,128)(2,1)S(1)}, u32[]{:S(2)}, u32[]{:S(2)}) collective-permute-start(bf16[192,512]{1,0:T(8,128)(2,1)S(1)} %get-tuple-element.14), channel_id=1, source_target_pairs={{0,6},{2,4},{4,2},{6,0},{1,7},{3,5},{5,3},{7,1},{8,14},{10,12},{12... | collective-permute-start | bytes 589832 | tf_op jit(solution)/shard_map/ppermute | solution.py:242
  136.6 3.9 %collective-permute-start.2 = (bf16[192,512]{1,0:T(8,128)(2,1)S(1)}, bf16[192,512]{1,0:T(8,128)(2,1)S(1)}, u32[]{:S(2)}, u32[]{:S(2)}) collective-permute-start(bf16[192,512]{1,0:T(8,128)(2,1)S(1)} %get-tuple-element.15), channel_id=1, source_target_pairs={{0,4},{2,6},{4,0},{6,2},{1,5},{3,7},{5,1},{7,3},{8,12},{10,14},{12... | collective-permute-start | bytes 589832 | tf_op jit(solution)/shard_map/ppermute | solution.py:242
  140.5 1.9 %collective-permute-start.3 = (bf16[192,512]{1,0:T(8,128)(2,1)S(1)}, bf16[192,512]{1,0:T(8,128)(2,1)S(1)}, u32[]{:S(2)}, u32[]{:S(2)}) collective-permute-start(bf16[192,512]{1,0:T(8,128)(2,1)S(1)} %get-tuple-element.16), channel_id=1, source_target_pairs={{0,2},{2,0},{4,6},{6,4},{1,3},{3,1},{5,7},{7,5},{8,10},{10,8},{12,... | collective-permute-start | bytes 589832 | tf_op jit(solution)/shard_map/ppermute | solution.py:242
  142.4 0.6 collective-permute-done.1
  143.0 13.3 %collective-permute-done.2 = bf16[192,512]{1,0:T(8,128)(2,1)S(1)} collective-permute-done((bf16[192,512]{1,0:T(8,128)(2,1)S(1)}, bf16[192,512]{1,0:T(8,128)(2,1)S(1)}, u32[]{:S(2)}, u32[]{:S(2)}) %collective-permute-start.2) | collective-permute-done | bytes 196640 | tf_op jit(solution)/shard_map/ppermute | solution.py:242
  156.3 0.0 collective-permute-done.3
  156.3 0.8 add_convert_fusion
  (12 shorter events, 0.0 us)
Async XLA Ops:
  0.0 92.0 %copy-start.1 = (bf16[512,512]{1,0:T(8,128)(2,1)S(1)}, bf16[512,512]{1,0:T(8,128)(2,1)}, u32[]{:S(2)}) copy-start(bf16[512,512]{1,0:T(8,128)(2,1)} %constant.10.clone.mid_ref) | copy-start | bytes 1572868
  0.0 92.0 %copy-start.6 = (bf16[256,64]{1,0:T(8,128)(2,1)S(1)}, bf16[256,64]{1,0:T(8,128)(2,1)}, u32[]{:S(2)}) copy-start(bf16[256,64]{1,0:T(8,128)(2,1)} %constant.8.clone.fwd_ref) | copy-start | bytes 98308
  0.0 92.0 %copy-start.7 = (bf16[64,256]{1,0:T(8,128)(2,1)S(1)}, bf16[64,256]{1,0:T(8,128)(2,1)}, u32[]{:S(2)}) copy-start(bf16[64,256]{1,0:T(8,128)(2,1)} %constant.9.clone.back_ref) | copy-start | bytes 98308
  2.4 89.5 %all-to-all-start = ((bf16[64,8,512]{2,1,0:T(8,128)(2,1)}), bf16[64,8,512]{2,1,0:T(8,128)(2,1)S(1)}, u32[]{:S(2)}, u32[]{:S(2)}) async-start(bf16[64,8,512]{2,1,0:T(8,128)(2,1)} %shard_map.100), calls=%async_computation | async-start | bytes 1048576 | tf_op jit(solution)/shard_map/all_to_all | solution.py:216
  24.2 104.0 %copy-start.2 = (bf16[192,256]{1,0:T(8,128)(2,1)S(1)}, bf16[192,256]{1,0:T(8,128)(2,1)}, u32[]{:S(2)}) copy-start(bf16[192,256]{1,0:T(8,128)(2,1)} %k_ref.1) | copy-start | bytes 294916
  24.2 103.9 %copy-start.3 = (bf16[192,256]{1,0:T(8,128)(2,1)S(1)}, bf16[192,256]{1,0:T(8,128)(2,1)}, u32[]{:S(2)}) copy-start(bf16[192,256]{1,0:T(8,128)(2,1)} %v_ref.1) | copy-start | bytes 294916
  24.2 103.9 %copy-start.5 = (bf16[192,256]{1,0:T(8,128)(2,1)S(1)}, bf16[192,256]{1,0:T(8,128)(2,1)}, u32[]{:S(2)}) copy-start(bf16[192,256]{1,0:T(8,128)(2,1)} %q_ref.1) | copy-start | bytes 294916
  24.2 103.9 %copy-start.8 = (f32[256]{0:T(256)S(1)}, f32[256]{0:T(256)}, u32[]{:S(2)}) copy-start(f32[256]{0:T(256)} %param.14) | copy-start | bytes 3076
  89.0 43.6 %copy-start = (bf16[4,256,512]{2,1,0:T(8,128)(2,1)S(1)}, bf16[4,256,512]{2,1,0:T(8,128)(2,1)}, u32[]{:S(2)}) copy-start(bf16[4,256,512]{2,1,0:T(8,128)(2,1)} %get-tuple-element.11.mine_ref) | copy-start | bytes 3145732
  89.0 43.6 %collective-permute-start = (bf16[4,256,512]{2,1,0:T(8,128)(2,1)}, bf16[4,256,512]{2,1,0:T(8,128)(2,1)S(1)}, u32[]{:S(2)}, u32[]{:S(2)}) collective-permute-start(bf16[4,256,512]{2,1,0:T(8,128)(2,1)} %get-tuple-element.12), channel_id=1, source_target_pairs={{0,1},{1,0},{2,3},{3,2},{4,5},{5,4},{6,7},{7,6},{8,9},{9,8},{10,11... | collective-permute-start | bytes 3145736 | tf_op jit(solution)/shard_map/ppermute | solution.py:225
  92.0 1.0 copy-start.4
  133.1 9.9 %collective-permute-start.1 = (bf16[192,512]{1,0:T(8,128)(2,1)S(1)}, bf16[192,512]{1,0:T(8,128)(2,1)S(1)}, u32[]{:S(2)}, u32[]{:S(2)}) collective-permute-start(bf16[192,512]{1,0:T(8,128)(2,1)S(1)} %get-tuple-element.14), channel_id=1, source_target_pairs={{0,6},{2,4},{4,2},{6,0},{1,7},{3,5},{5,3},{7,1},{8,14},{10,12},{12... | collective-permute-start | bytes 589832 | tf_op jit(solution)/shard_map/ppermute | solution.py:242
  136.6 19.7 %collective-permute-start.2 = (bf16[192,512]{1,0:T(8,128)(2,1)S(1)}, bf16[192,512]{1,0:T(8,128)(2,1)S(1)}, u32[]{:S(2)}, u32[]{:S(2)}) collective-permute-start(bf16[192,512]{1,0:T(8,128)(2,1)S(1)} %get-tuple-element.15), channel_id=1, source_target_pairs={{0,4},{2,6},{4,0},{6,2},{1,5},{3,7},{5,1},{7,3},{8,12},{10,14},{12... | collective-permute-start | bytes 589832 | tf_op jit(solution)/shard_map/ppermute | solution.py:242
  140.5 15.8 %collective-permute-start.3 = (bf16[192,512]{1,0:T(8,128)(2,1)S(1)}, bf16[192,512]{1,0:T(8,128)(2,1)S(1)}, u32[]{:S(2)}, u32[]{:S(2)}) collective-permute-start(bf16[192,512]{1,0:T(8,128)(2,1)S(1)} %get-tuple-element.16), channel_id=1, source_target_pairs={{0,2},{2,0},{4,6},{6,4},{1,3},{3,1},{5,7},{7,5},{8,10},{10,8},{12,... | collective-permute-start | bytes 589832 | tf_op jit(solution)/shard_map/ppermute | solution.py:242

commit v4 on v3

v4 whole, which is shorter than its diff:
```python
import math

import jax
import jax.numpy as jnp
import numpy as np
from jax import lax
from jax.experimental import pallas as pl
from jax.experimental.pallas import tpu as pltpu
from jax.sharding import Mesh
from jax.sharding import PartitionSpec as P

CTX = ("x", "zh", "y")
LANES = 128
BLOCK = 256
CHANS = 4
TOKENS = 192
F32, BF16 = jnp.float32, jnp.bfloat16


def tables(groups):
    rows, length = 2 * groups, 2 * groups * TOKENS
    kb = (np.arange(2)[:, None] + 2 * np.arange(groups)[None, :]).reshape(-1)
    n1, n2 = np.arange(groups), np.arange(TOKENS)
    first = 2.0 * math.pi * (np.outer(n1, kb) % rows) / rows
    middle = 2.0 * math.pi * (np.outer(n2, n2) % TOKENS) / TOKENS
    turn = 2.0 * math.pi * (np.outer(kb, n2) % length) / length
    ends = np.concatenate([np.cos(first), -np.sin(first)], axis=1)
    pad = ((0, 0), (0, BLOCK - TOKENS))
    cos_m, sin_m = (np.pad(f(middle), (pad[1], pad[1])) for f in (np.cos, np.sin))
    return jnp.asarray(
        np.concatenate(
            [
                np.block([[cos_m, -sin_m], [sin_m, cos_m]]),
                np.concatenate([np.pad(np.cos(turn), pad), np.pad(np.sin(turn), pad)], axis=1),
                np.concatenate([ends, ends / length], axis=1),
            ]
        ),
        BF16,
    )


def dot(a, b, dims=((1,), (0,))):
    return lax.dot_general(a, b, (dims, ((), ())), preferred_element_type=F32)


def low_half(shape):
    return lax.broadcasted_iota(jnp.int32, shape, 0) % 8 < 4


def pack_kernel(k_hbm, v_hbm, h_hbm, out_ref, mixed_ref, k_ref, v_ref, h_ref, sems):
    pairs = [(h_hbm.at[i], h_ref.at[i]) for i in range(4)] + [(k_hbm, k_ref), (v_hbm, v_ref)]
    copies = [pltpu.make_async_copy(a, b, sems.at[i]) for i, (a, b) in enumerate(pairs)]
    for i in (0, 2, 4, 5, 1, 3):
        copies[i].start()
    half, rest = LANES, TOKENS - LANES

    def column(j):
        if j == 0:
            rows = mixed_ref[pl.ds(0, half), :].astype(F32)
        elif j == 1:
            rows = jnp.concatenate(
                [mixed_ref[pl.ds(half, rest), :].astype(F32), h_ref[3, pl.ds(0, rest), :]], axis=0
            )
        elif j % 2 == 0:
            rows = h_ref[j // 2 - 1, pl.ds(0, half), :]
        else:
            last = h_ref[j // 2 - 1, pl.ds(half, rest), :]
            if j < 7:
                more = h_ref[3, pl.ds(rest * (j // 2), rest), :]
            else:
                more = pltpu.roll(last, last.shape[1] - 2, axis=1)
            rows = jnp.concatenate([last, more], axis=0)
        return rows.T

    def tile(j):
        a, b = column(j), column(j + 4)
        channels = a.shape[0]
        low = low_half(a.shape)
        even = jnp.where(low, a, pltpu.roll(b, 4, axis=0))
        odd = jnp.where(low, pltpu.roll(a, channels - 4, axis=0), b)
        both = jnp.stack(
            [even.reshape(channels // 8, 8, LANES), odd.reshape(channels // 8, 8, LANES)], axis=1
        )
        return both.reshape(channels // 4, 8, LANES)

    tiles = [None] * 4
    for j, needs in ((2, (0, 2)), (0, (4, 5, 1)), (1, (3,)), (3, ())):
        for i in needs:
            copies[i].wait()
        if j == 0:
            mixed_ref[...] = (k_ref[...].astype(F32) * v_ref[...].astype(F32)).astype(BF16)
        tiles[j] = tile(j)
    out_ref[...] = jnp.concatenate(tiles, axis=1)[:, : out_ref.shape[1]].astype(BF16)


def conv_kernel(got_ref, table_ref, out_ref, wide_ref, flat_ref):
    groups = got_ref.shape[0]
    rows = 2 * groups
    got = got_ref[...].astype(F32)
    for j in range(4):
        rows_j = got[:, 8 * j : 8 * j + 8]
        short = 8 - rows_j.shape[1]
        if short:
            rows_j = jnp.concatenate([rows_j, jnp.zeros((groups, short, LANES), F32)], axis=1)
        wide_ref[j] = rows_j.reshape(8 * groups, LANES)
    lower = lax.broadcasted_iota(jnp.int32, (groups, LANES), 1) < TOKENS - LANES
    shift = TOKENS - LANES

    def load(c, j):
        return wide_ref[j % 4, pl.ds(CHANS * (j // 4) + c, groups, stride=8), :]

    mid = table_ref[pl.ds(0, 2 * BLOCK), :]
    turn = table_ref[pl.ds(2 * BLOCK, rows), :].astype(F32)
    ends = table_ref[pl.ds(2 * BLOCK + rows, groups), :]
    tc, ts = turn[:, :BLOCK], turn[:, BLOCK:]
    signal, filt = [], []
    for c in range(CHANS):
        t = [load(c, j) for j in range(7)] + [load(c % 2, 7)]
        if c >= 2:
            t[7] = pltpu.roll(t[7], shift, axis=1)
        signal.append(jnp.concatenate([t[0], t[1]], axis=1))
        third = jnp.where(lower, pltpu.roll(t[1], shift, axis=1), t[3])
        hr = jnp.concatenate(
            [jnp.concatenate([t[2], t[3]], axis=1), jnp.concatenate([t[4], t[5]], axis=1)], axis=0
        )
        hi = jnp.concatenate(
            [
                jnp.concatenate([t[6], t[7]], axis=1),
                jnp.concatenate([third, pltpu.roll(t[5], shift, axis=1)], axis=1),
            ],
            axis=0,
        )
        filt.append((hr, hi))
    a = dot(ends[:, :BLOCK], jnp.concatenate(signal, axis=1).astype(BF16), ((0,), (0,)))
    turned = []
    for c in range(CHANS):
        re, im = a[:rows, c * BLOCK : (c + 1) * BLOCK], a[rows:, c * BLOCK : (c + 1) * BLOCK]
        turned.append(jnp.concatenate([re * tc + im * ts, im * tc - re * ts], axis=1).astype(BF16))
    b = dot(jnp.concatenate(turned, axis=0), mid)
    product = []
    for c in range(CHANS):
        re, im = b[c * rows : (c + 1) * rows, :BLOCK], b[c * rows : (c + 1) * rows, BLOCK:]
        hr, hi = filt[c]
        product.append(jnp.concatenate([re * hr - im * hi, re * hi + im * hr], axis=1).astype(BF16))
    g = dot(jnp.concatenate(product, axis=0), mid, ((1,), (1,)))
    turned = []
    for c in range(CHANS):
        re, im = g[c * rows : (c + 1) * rows, :BLOCK], g[c * rows : (c + 1) * rows, BLOCK:]
        turned.append(jnp.concatenate([re * tc - im * ts, im * tc + re * ts], axis=0).astype(BF16))
    y = dot(ends[:, BLOCK:], jnp.concatenate(turned, axis=1))
    for c in range(CHANS):
        flat_ref[pl.ds(c, groups, stride=8), :] = y[:, c * BLOCK : c * BLOCK + LANES]
    for c in range(2):
        one, two = (y[:, e * BLOCK + LANES : (e + 1) * BLOCK] for e in (c, c + 2))
        pair = jnp.where(lower, one, pltpu.roll(two, shift, axis=1))
        flat_ref[pl.ds(CHANS + c, groups, stride=8), :] = pair
        flat_ref[pl.ds(CHANS + 2 + c, groups, stride=8), :] = jnp.zeros_like(pair)
    out = flat_ref[...].reshape(groups, 8, LANES)
    out_ref[...] = out[:, : out_ref.shape[1]].astype(BF16)


def gate_kernel(got_ref, q_ref, mixed_ref, skip_ref, out_ref):
    groups, height, _ = got_ref.shape
    got = got_ref[...].astype(F32)
    got = jnp.concatenate([got, jnp.zeros((groups, 8 - height, LANES), F32)], axis=1)
    got = got.reshape(8 * groups, LANES)
    far = pltpu.roll(pltpu.roll(got, TOKENS - LANES, axis=1), 2, axis=0)
    row = lax.broadcasted_iota(jnp.int32, got.shape, 0) % 8
    tiles = jnp.where(row < 6, got, far).reshape(groups // 2, 2, 8, LANES)
    even = tiles[:, 0].reshape(4 * groups, LANES)
    odd = tiles[:, 1].reshape(4 * groups, LANES)
    low = low_half(even.shape)
    first = jnp.where(low, even, pltpu.roll(odd, 4, axis=0))
    second = jnp.where(low, pltpu.roll(even, 4 * groups - 4, axis=0), odd)
    conv = jnp.concatenate([first.T, second.T[: TOKENS - LANES]], axis=0)
    gated = q_ref[...].astype(F32) * (conv + skip_ref[...] * mixed_ref[...].astype(F32))
    out_ref[...] = gated.astype(BF16)


def split_kernel(w_hbm, mine_ref, other_ref, sems):
    core = lax.axis_index("core")
    lines, _, width = mine_ref.shape
    copies = []
    for line in range(lines):
        for side, (out, owner) in enumerate(((mine_ref, core), (other_ref, 1 - core))):
            start = pl.multiple_of((2 * line + owner) * width, LANES)
            copies.append(
                pltpu.make_async_copy(
                    w_hbm.at[:, pl.ds(start, width)], out.at[line], sems.at[2 * line + side]
                )
            )
    for copy in copies:
        copy.start()
    for copy in copies:
        copy.wait()


def project_kernel(near_ref, mine_ref, other_ref, out_ref):
    core = lax.axis_index("core")
    ours, theirs = near_ref[core], near_ref[1 - core]
    for dest in range(out_ref.shape[0]):
        out_ref[dest] = (dot(ours, mine_ref[dest]) + dot(theirs, other_ref[dest])).astype(BF16)


def call(kernel, shapes, args, scratch=(), hbm=False):
    many = isinstance(shapes, list)
    out_shape = [jax.ShapeDtypeStruct(s, BF16) for s in (shapes if many else [shapes])]
    extra = {}
    if not hbm:
        extra["compiler_params"] = pltpu.CompilerParams(vmem_limit_bytes=24 * 2**20)
    else:
        extra["in_specs"] = [pl.BlockSpec(memory_space=pltpu.HBM)] * len(args)
    out = pl.pallas_call(
        kernel,
        out_shape=out_shape,
        scratch_shapes=list(scratch),
        **extra,
    )(*args)
    return out if many else out[0]


def local(query_branch, key_branch, value_branch, spectrum, skip_gain, out_weight):
    groups = lax.axis_size(CTX)
    tokens, channels = query_branch.shape
    lines, cores = lax.axis_size("zl"), lax.axis_size("core")
    width = out_weight.shape[1] // (lines * cores)
    payload, mixed = call(
        pack_kernel,
        [(groups, 30, LANES), (tokens, channels)],
        (key_branch, value_branch, spectrum.reshape(4, tokens, channels)),
        [
            pltpu.VMEM((tokens, channels), BF16),
            pltpu.VMEM((tokens, channels), BF16),
            pltpu.VMEM((4, tokens, channels), F32),
            pltpu.SemaphoreType.DMA((6,)),
        ],
        hbm=True,
    )
    got = lax.all_to_all(payload, CTX, 0, 0, tiled=True)
    mine, other = call(
        split_kernel,
        [(lines, channels, width)] * 2,
        (out_weight,),
        [pltpu.SemaphoreType.DMA((2 * lines,))],
        hbm=True,
    )
    other = lax.ppermute(other, "core", [(0, 1), (1, 0)])
    y = call(
        conv_kernel,
        (groups, 6, LANES),
        (got, tables(groups)),
        [pltpu.VMEM((4, 8 * groups, LANES), F32), pltpu.VMEM((8 * groups, LANES), F32)],
    )
    y = lax.all_to_all(y, CTX, 0, 0, tiled=True)
    gated = call(
        gate_kernel,
        (tokens, channels),
        (y, query_branch, mixed, skip_gain.reshape(1, channels)),
    )
    near = lax.all_gather(gated, "core", axis=0)
    pieces = call(project_kernel, (lines, tokens, width), (near, mine, other))
    pieces = lax.all_to_all(pieces, "zl", 0, 0, tiled=True)
    return jnp.sum(pieces.astype(F32), axis=0).astype(BF16)


def solution(mesh):
    fine = Mesh(mesh.devices.reshape(4, 4, 4, 4, 2), ("x", "zh", "y", "zl", "core"))
    tp = ("zl", "core")
    placed = (
        P(CTX, tp),
        P(CTX, tp),
        P(CTX, tp),
        P(None, CTX, None, tp),
        P(tp),
        P(tp, None),
    )
    return jax.shard_map(local, mesh=fine, in_specs=placed, out_specs=P(CTX, tp), check_vma=False)
```

time: 157 us -> 112 us (0.71)
  Pallas kernels: 69 us -> 7.55 us
  blocking collectives: 38.2 us -> 56.3 us
  starting transfers between devices: 34 us -> 24.7 us
  waiting for transfers between devices: 13.9 us -> 21.7 us
    pallas_call x5, Pallas kernels: 69 us -> 7.55 us  [call(): pl.pallas_call(kernel, out_shape=out_shape, scratch_shapes=list(scratch),...]
    all_to_all x0 -> x1, blocking collectives: none -> 23 us  [local(): pieces = lax.all_to_all(pieces, 'zl', 0, 0, tiled=True)]
    all_to_all x1, waiting for transfers between devices: 0.01 us -> 21.7 us  [local(): got = lax.all_to_all(payload, CTX, 0, 0, tiled=True)]
    ppermute x3 -> x0, waiting for transfers between devices: 13.9 us -> none  [local(): back = lax.ppermute(pieces[d], 'zl', [(i, i ^ d) for i in range(lines)])]
    ppermute x3 -> x0, starting transfers between devices: 9.27 us -> none  [local(): back = lax.ppermute(pieces[d], 'zl', [(i, i ^ d) for i in range(lines)])]
    all_to_all x1, blocking collectives: 34 us -> 26.9 us  [local(): y = lax.all_to_all(y, CTX, 0, 0, tiled=True)]
    all_gather x1, blocking collectives: 4.25 us -> 6.36 us  [local(): near = lax.all_gather(gated, 'core', axis=0)]
  transfers between devices with their start and end apart: 5 -> 2, of which waited for: 2 -> 1; matrix products, arithmetic and copies ran while one was open for 0% -> 0% of each run, Pallas kernels for 42% -> 4%
where the time goes in v4:
time: 112 us; the launch traced here: 111 us
  blocking collectives  56.3 us (50%)
  starting transfers between devices  24.7 us (22%)
  waiting for transfers between devices  21.7 us (19%)
  Pallas kernels  7.55 us (7%)
    all_to_all x1, blocking collectives, local(): y = lax.all_to_all(y, CTX, 0, 0, tiled=True)  26.9 us
    all_to_all x1, blocking collectives, local(): pieces = lax.all_to_all(pieces, 'zl', 0, 0, tiled=True)  23 us
    all_to_all x1, starting transfers between devices, local(): got = lax.all_to_all(payload, CTX, 0, 0, tiled=True)  21.8 us
    all_to_all x1, waiting for transfers between devices, local(): got = lax.all_to_all(payload, CTX, 0, 0, tiled=True)  21.7 us
    pallas_call x5, Pallas kernels, call(): pl.pallas_call(kernel, out_shape=out_shape, scratch_shapes=list(scratch),...  7.55 us
    all_gather x1, blocking collectives, local(): near = lax.all_gather(gated, 'core', axis=0)  6.36 us
    ppermute x1, starting transfers between devices, local(): other = lax.ppermute(other, 'core', [(0, 1), (1, 0)])  2.99 us
  transfers between devices with their start and end apart: 2, of which 1 were waited for; matrix products, arithmetic and copies ran while one was open for 0% of the time, Pallas kernels for 4%

profile of v4, /device:TPU:1, one launch (start us, length us, event | category | flops | bytes accessed | tf_op | source)
XLA Modules:
  0.0 111.2 jit_solution(12883254310988044235)
XLA Ops:
  0.0 0.0 copy-start.1
  0.0 2.5 %shard_map.73 = (bf16[64,30,128]{2,1,0:T(8,128)(2,1)}, bf16[192,256]{1,0:T(8,128)(2,1)}) custom-call(bf16[192,256]{1,0:T(8,128)(2,1)} %k_hbm.1, bf16[192,256]{1,0:T(8,128)(2,1)} %v_hbm.1, f32[4,192,256]{2,1,0:T(8,128)} %bitcast.5), custom_call_target="tpu_custom_call" | custom-call | tf_op jit(solution)/shard_map/pallas_call | solution.py:213
  2.5 21.8 %all-to-all-start = ((bf16[64,30,128]{2,1,0:T(8,128)(2,1)}), bf16[64,30,128]{2,1,0:T(8,128)(2,1)S(1)}, u32[]{:S(2)}, u32[]{:S(2)}) async-start(bf16[64,30,128]{2,1,0:T(8,128)(2,1)} %get-tuple-element.9), calls=%async_computation | async-start | bytes 1048576 | tf_op jit(solution)/shard_map/all_to_all | solution.py:239
  24.2 0.0 copy-start.2
  24.3 0.0 copy-start.3
  24.3 0.0 copy-start.4
  24.3 3.0 %shard_map.76 = (bf16[4,256,512]{2,1,0:T(8,128)(2,1)}, bf16[4,256,512]{2,1,0:T(8,128)(2,1)}) custom-call(bf16[256,4096]{1,0:T(8,128)(2,1)} %w_hbm.1), custom_call_target="tpu_custom_call" | custom-call | tf_op jit(solution)/shard_map/pallas_call | solution.py:213
  27.3 0.0 copy-start
  27.3 3.0 %collective-permute-start = (bf16[4,256,512]{2,1,0:T(8,128)(2,1)}, bf16[4,256,512]{2,1,0:T(8,128)(2,1)S(1)}, u32[]{:S(2)}, u32[]{:S(2)}) collective-permute-start(bf16[4,256,512]{2,1,0:T(8,128)(2,1)} %get-tuple-element.12), channel_id=1, source_target_pairs={{0,1},{1,0},{2,3},{3,2},{4,5},{5,4},{6,7},{7,6},{8,9},{9,8},{10,11... | collective-permute-start | bytes 3145736 | tf_op jit(solution)/shard_map/ppermute | solution.py:247
  30.3 21.7 %all-to-all-done.got_ref = bf16[64,30,128]{2,1,0:T(8,128)(2,1)S(1)} async-done(((bf16[64,30,128]{2,1,0:T(8,128)(2,1)}), bf16[64,30,128]{2,1,0:T(8,128)(2,1)S(1)}, u32[]{:S(2)}, u32[]{:S(2)}) %all-to-all-start) | async-done | bytes 491552 | tf_op jit(solution)/shard_map/all_to_all | solution.py:239
  52.0 0.0 copy-done.1
  52.0 1.3 %shard_map.74 = bf16[64,6,128]{2,1,0:T(8,128)(2,1)S(1)} custom-call(bf16[64,30,128]{2,1,0:T(8,128)(2,1)S(1)} %all-to-all-done.got_ref, bf16[704,512]{1,0:T(8,128)(2,1)S(1)} %copy-done.1), custom_call_target="tpu_custom_call" | custom-call | tf_op jit(solution)/shard_map/pallas_call | solution.py:213
  53.3 26.9 %all_to_all.15.got_ref = bf16[64,6,128]{2,1,0:T(8,128)(2,1)S(1)} all-to-all(bf16[64,6,128]{2,1,0:T(8,128)(2,1)S(1)} %shard_map.74), channel_id=1, replica_groups=mesh['x'=4,'zh'=4,'y'=4,'zl'=4,'core'=2] {'x','zh','y'}, dimensions={0} | all-to-all | bytes 196608 | tf_op jit(solution)/shard_map/all_to_all | solution.py:254
  80.2 0.0 copy-done.2
  80.2 0.0 copy-done.3
  80.2 0.0 copy-done.4
  80.2 0.2 shard_map.75
  80.4 6.4 %all-gather = bf16[384,256]{1,0:T(8,128)(2,1)S(1)} all-gather(bf16[192,256]{1,0:T(8,128)(2,1)S(1)} %shard_map.75), channel_id=2, replica_groups=mesh['x'=4,'zh'=4,'y'=4,'zl'=4,'core'=2] {'core'}, dimensions={0}, use_global_device_ids=true | all-gather | bytes 294912 | tf_op jit(solution)/shard_map/all_gather | solution.py:260
  86.8 0.0 collective-permute-done.other_ref
  86.8 0.0 copy-done
  86.8 0.6 shard_map.77
  87.4 23.0 %all_to_all.16 = bf16[4,192,512]{2,1,0:T(8,128)(2,1)S(1)} all-to-all(bf16[4,192,512]{2,1,0:T(8,128)(2,1)S(1)} %shard_map.77), channel_id=1, replica_groups=mesh['x'=4,'zh'=4,'y'=4,'zl'=4,'core'=2] {'zl'}, dimensions={0} | all-to-all | bytes 1572864 | tf_op jit(solution)/shard_map/all_to_all | solution.py:262
  110.4 0.8 reduce_sum.12
Async XLA Ops:
  0.0 52.0 %copy-start.1 = (bf16[704,512]{1,0:T(8,128)(2,1)S(1)}, bf16[704,512]{1,0:T(8,128)(2,1)}, u32[]{:S(2)}) copy-start(bf16[704,512]{1,0:T(8,128)(2,1)} %constant.5.clone.table_ref) | copy-start | bytes 2162692
  2.5 49.5 %all-to-all-start = ((bf16[64,30,128]{2,1,0:T(8,128)(2,1)}), bf16[64,30,128]{2,1,0:T(8,128)(2,1)S(1)}, u32[]{:S(2)}, u32[]{:S(2)}) async-start(bf16[64,30,128]{2,1,0:T(8,128)(2,1)} %get-tuple-element.9), calls=%async_computation | async-start | bytes 1048576 | tf_op jit(solution)/shard_map/all_to_all | solution.py:239
  24.2 56.0 %copy-start.2 = (bf16[192,256]{1,0:T(8,128)(2,1)S(1)}, bf16[192,256]{1,0:T(8,128)(2,1)}, u32[]{:S(2)}) copy-start(bf16[192,256]{1,0:T(8,128)(2,1)} %q_ref.1) | copy-start | bytes 294916
  24.3 55.9 %copy-start.3 = (bf16[192,256]{1,0:T(8,128)(2,1)S(1)}, bf16[192,256]{1,0:T(8,128)(2,1)}, u32[]{:S(2)}) copy-start(bf16[192,256]{1,0:T(8,128)(2,1)} %get-tuple-element.10.mixed_ref) | copy-start | bytes 294916
  24.3 55.9 %copy-start.4 = (f32[256]{0:T(256)S(1)}, f32[256]{0:T(256)}, u32[]{:S(2)}) copy-start(f32[256]{0:T(256)} %param.11) | copy-start | bytes 3076
  27.3 59.5 %copy-start = (bf16[4,256,512]{2,1,0:T(8,128)(2,1)S(1)}, bf16[4,256,512]{2,1,0:T(8,128)(2,1)}, u32[]{:S(2)}) copy-start(bf16[4,256,512]{2,1,0:T(8,128)(2,1)} %get-tuple-element.11.mine_ref) | copy-start | bytes 3145732
  27.3 59.5 %collective-permute-start = (bf16[4,256,512]{2,1,0:T(8,128)(2,1)}, bf16[4,256,512]{2,1,0:T(8,128)(2,1)S(1)}, u32[]{:S(2)}, u32[]{:S(2)}) collective-permute-start(bf16[4,256,512]{2,1,0:T(8,128)(2,1)} %get-tuple-element.12), channel_id=1, source_target_pairs={{0,1},{1,0},{2,3},{3,2},{4,5},{5,4},{6,7},{7,6},{8,9},{9,8},{10,11... | collective-permute-start | bytes 3145736 | tf_op jit(solution)/shard_map/ppermute | solution.py:247

commit v5 on v4

--- a/solution.py
+++ b/solution.py
@@ -1,3 +1,4 @@
+import functools
 import math
 
 import jax
@@ -195,11 +196,23 @@
         copy.wait()
 
 
-def project_kernel(near_ref, mine_ref, other_ref, out_ref):
-    core = lax.axis_index("core")
+def project_kernel(half, near_ref, mine_ref, other_ref, send_ref, keep_ref):
+    core, line = lax.axis_index("core"), lax.axis_index("zl")
     ours, theirs = near_ref[core], near_ref[1 - core]
-    for dest in range(out_ref.shape[0]):
-        out_ref[dest] = (dot(ours, mine_ref[dest]) + dot(theirs, other_ref[dest])).astype(BF16)
+    width = send_ref.shape[-1]
+    columns = pl.ds(half * width, width)
+    for d, out in ((1, send_ref.at[0]), (3, send_ref.at[1]), (2, keep_ref.at[1]), (0, keep_ref.at[0])):
+        dest = line ^ d
+        total = dot(ours, mine_ref[dest, :, columns]) + dot(theirs, other_ref[dest, :, columns])
+        out[...] = total.astype(BF16)
+
+
+def finish_kernel(*refs):
+    out_ref = refs[-1]
+    halves = [refs[i : i + 3] for i in range(0, len(refs) - 1, 3)]
+    for half, (keep, back, far) in enumerate(halves):
+        total = keep[0].astype(F32) + back[0].astype(F32) + far[...].astype(F32)
+        out_ref[:, pl.ds(half * far.shape[1], far.shape[1])] = total.astype(BF16)
 
 
 def call(kernel, shapes, args, scratch=(), hbm=False):
@@ -258,9 +271,22 @@
         (y, query_branch, mixed, skip_gain.reshape(1, channels)),
     )
     near = lax.all_gather(gated, "core", axis=0)
-    pieces = call(project_kernel, (lines, tokens, width), (near, mine, other))
-    pieces = lax.all_to_all(pieces, "zl", 0, 0, tiled=True)
-    return jnp.sum(pieces.astype(F32), axis=0).astype(BF16)
+    def trade(value, d):
+        return lax.ppermute(value, "zl", [(i, i ^ d) for i in range(lines)])
+
+    parts = 2
+    shape = (2, tokens, width // parts)
+    first = []
+    for half in range(parts):
+        send, keep = call(
+            functools.partial(project_kernel, half), [shape, shape], (near, mine, other)
+        )
+        first.append((keep, trade(send, 1)))
+    shares = []
+    for keep, back in first:
+        far = (keep[1].astype(F32) + back[1].astype(F32)).astype(BF16)
+        shares += [keep, back, trade(far, 2)]
+    return call(finish_kernel, (tokens, width), shares)
 
 
 def solution(mesh):

time: 112 us -> 109 us (0.973)
  blocking collectives: 56.3 us -> 33.3 us
  starting transfers between devices: 24.7 us -> 37.5 us
  waiting for transfers between devices: 21.7 us -> 29.5 us
    all_to_all x1 -> x0, blocking collectives: 23 us -> none  [local(): pieces = lax.all_to_all(pieces, 'zl', 0, 0, tiled=True)]
    ppermute x0 -> x4, starting transfers between devices: none -> 12.8 us  [trade(): return lax.ppermute(value, 'zl', [(i, i ^ d) for i in range(lines)])]
    ppermute x0 -> x4, waiting for transfers between devices: none -> 7.76 us  [trade(): return lax.ppermute(value, 'zl', [(i, i ^ d) for i in range(lines)])]
    pallas_call x5 -> x7, Pallas kernels: 7.55 us -> 8.49 us  [call(): pl.pallas_call(kernel, out_shape=out_shape, scratch_shapes=list(scratch),...]
  transfers between devices with their start and end apart: 2 -> 6, of which waited for: 1 -> 4; matrix products, arithmetic and copies ran while one was open for 0% -> 0% of each run, Pallas kernels for 4% -> 4%
where the time goes in v5:
time: 109 us
  starting transfers between devices  37.5 us (34%)
  blocking collectives  33.3 us (31%)
  waiting for transfers between devices  29.5 us (27%)
  Pallas kernels  8.49 us (8%)
    all_to_all x1, blocking collectives, local(): y = lax.all_to_all(y, CTX, 0, 0, tiled=True)  26.9 us
    all_to_all x1, starting transfers between devices, local(): got = lax.all_to_all(payload, CTX, 0, 0, tiled=True)  21.8 us
    all_to_all x1, waiting for transfers between devices, local(): got = lax.all_to_all(payload, CTX, 0, 0, tiled=True)  21.7 us
    ppermute x4, starting transfers between devices, trade(): return lax.ppermute(value, 'zl', [(i, i ^ d) for i in range(lines)])  12.8 us
    pallas_call x7, Pallas kernels, call(): pl.pallas_call(kernel, out_shape=out_shape, scratch_shapes=list(scratch),...  8.49 us
    ppermute x4, waiting for transfers between devices, trade(): return lax.ppermute(value, 'zl', [(i, i ^ d) for i in range(lines)])  7.76 us
    all_gather x1, blocking collectives, local(): near = lax.all_gather(gated, 'core', axis=0)  6.36 us
    ppermute x1, starting transfers between devices, local(): other = lax.ppermute(other, 'core', [(0, 1), (1, 0)])  2.99 us
  transfers between devices with their start and end apart: 6, of which 4 were waited for; matrix products, arithmetic and copies ran while one was open for 0% of the time, Pallas kernels for 4%

profile of v5, /device:TPU:1, one launch (start us, length us, event | category | flops | bytes accessed | tf_op | source)
XLA Modules:
  0.0 108.9 jit_solution(55241679754843554)
XLA Ops:
  0.0 2.5 %shard_map.73 = (bf16[64,30,128]{2,1,0:T(8,128)(2,1)}, bf16[192,256]{1,0:T(8,128)(2,1)}) custom-call(bf16[192,256]{1,0:T(8,128)(2,1)} %k_hbm.1, bf16[192,256]{1,0:T(8,128)(2,1)} %v_hbm.1, f32[4,192,256]{2,1,0:T(8,128)} %bitcast.10), custom_call_target="tpu_custom_call" | custom-call | tf_op jit(solution)/shard_map/pallas_call | solution.py:226
  2.5 21.8 %all-to-all-start = ((bf16[64,30,128]{2,1,0:T(8,128)(2,1)}), bf16[64,30,128]{2,1,0:T(8,128)(2,1)S(1)}, u32[]{:S(2)}, u32[]{:S(2)}) async-start(bf16[64,30,128]{2,1,0:T(8,128)(2,1)} %get-tuple-element.13), calls=%async_computation | async-start | bytes 1048576 | tf_op jit(solution)/shard_map/all_to_all | solution.py:252
  24.2 0.0 copy-start.2
  24.3 0.0 copy-start.3
  24.3 0.0 copy-start.4
  24.3 3.0 %shard_map.76 = (bf16[4,256,512]{2,1,0:T(8,128)(2,1)}, bf16[4,256,512]{2,1,0:T(8,128)(2,1)}) custom-call(bf16[256,4096]{1,0:T(8,128)(2,1)} %w_hbm.1), custom_call_target="tpu_custom_call" | custom-call | tf_op jit(solution)/shard_map/pallas_call | solution.py:226
  27.3 3.0 %collective-permute-start = (bf16[4,256,512]{2,1,0:T(8,128)(2,1)}, bf16[4,256,512]{2,1,0:T(8,128)(2,1)S(1)}, u32[]{:S(2)}, u32[]{:S(2)}) collective-permute-start(bf16[4,256,512]{2,1,0:T(8,128)(2,1)} %get-tuple-element.16), channel_id=1, source_target_pairs={{0,1},{1,0},{2,3},{3,2},{4,5},{5,4},{6,7},{7,6},{8,9},{9,8},{10,11... | collective-permute-start | bytes 3145736 | tf_op jit(solution)/shard_map/ppermute | solution.py:260
  30.3 21.7 %all-to-all-done.got_ref = bf16[64,30,128]{2,1,0:T(8,128)(2,1)S(1)} async-done(((bf16[64,30,128]{2,1,0:T(8,128)(2,1)}), bf16[64,30,128]{2,1,0:T(8,128)(2,1)S(1)}, u32[]{:S(2)}, u32[]{:S(2)}) %all-to-all-start) | async-done | bytes 491552 | tf_op jit(solution)/shard_map/all_to_all | solution.py:252
  52.0 1.3 %shard_map.74 = bf16[64,6,128]{2,1,0:T(8,128)(2,1)S(1)} custom-call(bf16[64,30,128]{2,1,0:T(8,128)(2,1)S(1)} %all-to-all-done.got_ref, bf16[704,512]{1,0:T(8,128)(2,1)S(1)} %copy-done.1), custom_call_target="tpu_custom_call" | custom-call | tf_op jit(solution)/shard_map/pallas_call | solution.py:226
  53.3 26.9 %all_to_all.10.got_ref = bf16[64,6,128]{2,1,0:T(8,128)(2,1)S(1)} all-to-all(bf16[64,6,128]{2,1,0:T(8,128)(2,1)S(1)} %shard_map.74), channel_id=1, replica_groups=mesh['x'=4,'zh'=4,'y'=4,'zl'=4,'core'=2] {'x','zh','y'}, dimensions={0} | all-to-all | bytes 196608 | tf_op jit(solution)/shard_map/all_to_all | solution.py:267
  80.2 0.2 shard_map.75
  80.4 6.4 %all-gather = bf16[384,256]{1,0:T(8,128)(2,1)S(1)} all-gather(bf16[192,256]{1,0:T(8,128)(2,1)S(1)} %shard_map.75), channel_id=2, replica_groups=mesh['x'=4,'zh'=4,'y'=4,'zl'=4,'core'=2] {'core'}, dimensions={0}, use_global_device_ids=true | all-gather | bytes 294912 | tf_op jit(solution)/shard_map/all_gather | solution.py:273
  86.8 0.0 collective-permute-done.other_ref
  86.8 0.4 shard_map.78
  87.2 3.9 %collective-permute-start.3 = (bf16[2,192,256]{2,1,0:T(8,128)(2,1)S(1)}, bf16[2,192,256]{2,1,0:T(8,128)(2,1)S(1)}, u32[]{:S(2)}, u32[]{:S(2)}) collective-permute-start(bf16[2,192,256]{2,1,0:T(8,128)(2,1)S(1)} %get-tuple-element.20), channel_id=1, source_target_pairs={{0,2},{2,0},{4,6},{6,4},{1,3},{3,1},{5,7},{7,5},{8,10},{10,8},{12,... | collective-permute-start | bytes 589832 | tf_op jit(solution)/shard_map/ppermute | solution.py:275
  91.1 0.4 shard_map.77
  91.5 1.9 %collective-permute-start.1 = (bf16[2,192,256]{2,1,0:T(8,128)(2,1)S(1)}, bf16[2,192,256]{2,1,0:T(8,128)(2,1)S(1)}, u32[]{:S(2)}, u32[]{:S(2)}) collective-permute-start(bf16[2,192,256]{2,1,0:T(8,128)(2,1)S(1)} %get-tuple-element.18), channel_id=1, source_target_pairs={{0,2},{2,0},{4,6},{6,4},{1,3},{3,1},{5,7},{7,5},{8,10},{10,8},{12,... | collective-permute-start | bytes 589832 | tf_op jit(solution)/shard_map/ppermute | solution.py:275
  93.4 2.6 %collective-permute-done.3.refs_4_ = bf16[2,192,256]{2,1,0:T(8,128)(2,1)S(1)} collective-permute-done((bf16[2,192,256]{2,1,0:T(8,128)(2,1)S(1)}, bf16[2,192,256]{2,1,0:T(8,128)(2,1)S(1)}, u32[]{:S(2)}, u32[]{:S(2)}) %collective-permute-start.3) | collective-permute-done | bytes 196640 | tf_op jit(solution)/shard_map/ppermute | solution.py:275
  96.1 3.4 %collective-permute-start.4 = (bf16[192,256]{1,0:T(8,128)(2,1)S(1)}, bf16[192,256]{1,0:T(8,128)(2,1)S(1)}, u32[]{:S(2)}, u32[]{:S(2)}) collective-permute-start(bf16[192,256]{1,0:T(8,128)(2,1)S(1)} %fusion.1), channel_id=1, source_target_pairs={{0,4},{2,6},{4,0},{6,2},{1,5},{3,7},{5,1},{7,3},{8,12},{10,14},{12... | collective-permute-start | bytes 294920 | tf_op jit(solution)/shard_map/ppermute | solution.py:275
  99.5 0.6 collective-permute-done.1.refs_1_
  100.1 3.6 %collective-permute-start.2 = (bf16[192,256]{1,0:T(8,128)(2,1)S(1)}, bf16[192,256]{1,0:T(8,128)(2,1)S(1)}, u32[]{:S(2)}, u32[]{:S(2)}) collective-permute-start(bf16[192,256]{1,0:T(8,128)(2,1)S(1)} %fusion), channel_id=1, source_target_pairs={{0,4},{2,6},{4,0},{6,2},{1,5},{3,7},{5,1},{7,3},{8,12},{10,14},{12... | collective-permute-start | bytes 294920 | tf_op jit(solution)/shard_map/ppermute | solution.py:275
  103.7 0.0 collective-permute-done.4.refs_5_
  103.7 4.5 %collective-permute-done.2.refs_2_ = bf16[192,256]{1,0:T(8,128)(2,1)S(1)} collective-permute-done((bf16[192,256]{1,0:T(8,128)(2,1)S(1)}, bf16[192,256]{1,0:T(8,128)(2,1)S(1)}, u32[]{:S(2)}, u32[]{:S(2)}) %collective-permute-start.2) | collective-permute-done | bytes 98336 | tf_op jit(solution)/shard_map/ppermute | solution.py:275
  108.2 0.7 shard_map.79
  (9 shorter events, 0.1 us)
Async XLA Ops:
  0.0 52.0 %copy-start.1 = (bf16[704,512]{1,0:T(8,128)(2,1)S(1)}, bf16[704,512]{1,0:T(8,128)(2,1)}, u32[]{:S(2)}) copy-start(bf16[704,512]{1,0:T(8,128)(2,1)} %constant.2.clone.table_ref) | copy-start | bytes 2162692
  2.5 49.5 %all-to-all-start = ((bf16[64,30,128]{2,1,0:T(8,128)(2,1)}), bf16[64,30,128]{2,1,0:T(8,128)(2,1)S(1)}, u32[]{:S(2)}, u32[]{:S(2)}) async-start(bf16[64,30,128]{2,1,0:T(8,128)(2,1)} %get-tuple-element.13), calls=%async_computation | async-start | bytes 1048576 | tf_op jit(solution)/shard_map/all_to_all | solution.py:252
  24.2 56.0 %copy-start.2 = (bf16[192,256]{1,0:T(8,128)(2,1)S(1)}, bf16[192,256]{1,0:T(8,128)(2,1)}, u32[]{:S(2)}) copy-start(bf16[192,256]{1,0:T(8,128)(2,1)} %q_ref.1) | copy-start | bytes 294916
  24.3 56.0 %copy-start.3 = (bf16[192,256]{1,0:T(8,128)(2,1)S(1)}, bf16[192,256]{1,0:T(8,128)(2,1)}, u32[]{:S(2)}) copy-start(bf16[192,256]{1,0:T(8,128)(2,1)} %get-tuple-element.14.mixed_ref) | copy-start | bytes 294916
  24.3 55.9 %copy-start.4 = (f32[256]{0:T(256)S(1)}, f32[256]{0:T(256)}, u32[]{:S(2)}) copy-start(f32[256]{0:T(256)} %param.11) | copy-start | bytes 3076
  27.3 59.5 %copy-start = (bf16[4,256,512]{2,1,0:T(8,128)(2,1)S(1)}, bf16[4,256,512]{2,1,0:T(8,128)(2,1)}, u32[]{:S(2)}) copy-start(bf16[4,256,512]{2,1,0:T(8,128)(2,1)} %get-tuple-element.15.mine_ref) | copy-start | bytes 3145732
  27.3 59.5 %collective-permute-start = (bf16[4,256,512]{2,1,0:T(8,128)(2,1)}, bf16[4,256,512]{2,1,0:T(8,128)(2,1)S(1)}, u32[]{:S(2)}, u32[]{:S(2)}) collective-permute-start(bf16[4,256,512]{2,1,0:T(8,128)(2,1)} %get-tuple-element.16), channel_id=1, source_target_pairs={{0,1},{1,0},{2,3},{3,2},{4,5},{5,4},{6,7},{7,6},{8,9},{9,8},{10,11... | collective-permute-start | bytes 3145736 | tf_op jit(solution)/shard_map/ppermute | solution.py:260
  87.2 8.9 %collective-permute-start.3 = (bf16[2,192,256]{2,1,0:T(8,128)(2,1)S(1)}, bf16[2,192,256]{2,1,0:T(8,128)(2,1)S(1)}, u32[]{:S(2)}, u32[]{:S(2)}) collective-permute-start(bf16[2,192,256]{2,1,0:T(8,128)(2,1)S(1)} %get-tuple-element.20), channel_id=1, source_target_pairs={{0,2},{2,0},{4,6},{6,4},{1,3},{3,1},{5,7},{7,5},{8,10},{10,8},{12,... | collective-permute-start | bytes 589832 | tf_op jit(solution)/shard_map/ppermute | solution.py:275
  91.5 8.6 %collective-permute-start.1 = (bf16[2,192,256]{2,1,0:T(8,128)(2,1)S(1)}, bf16[2,192,256]{2,1,0:T(8,128)(2,1)S(1)}, u32[]{:S(2)}, u32[]{:S(2)}) collective-permute-start(bf16[2,192,256]{2,1,0:T(8,128)(2,1)S(1)} %get-tuple-element.18), channel_id=1, source_target_pairs={{0,2},{2,0},{4,6},{6,4},{1,3},{3,1},{5,7},{7,5},{8,10},{10,8},{12,... | collective-permute-start | bytes 589832 | tf_op jit(solution)/shard_map/ppermute | solution.py:275
  96.1 7.6 %collective-permute-start.4 = (bf16[192,256]{1,0:T(8,128)(2,1)S(1)}, bf16[192,256]{1,0:T(8,128)(2,1)S(1)}, u32[]{:S(2)}, u32[]{:S(2)}) collective-permute-start(bf16[192,256]{1,0:T(8,128)(2,1)S(1)} %fusion.1), channel_id=1, source_target_pairs={{0,4},{2,6},{4,0},{6,2},{1,5},{3,7},{5,1},{7,3},{8,12},{10,14},{12... | collective-permute-start | bytes 294920 | tf_op jit(solution)/shard_map/ppermute | solution.py:275
  100.1 8.1 %collective-permute-start.2 = (bf16[192,256]{1,0:T(8,128)(2,1)S(1)}, bf16[192,256]{1,0:T(8,128)(2,1)S(1)}, u32[]{:S(2)}, u32[]{:S(2)}) collective-permute-start(bf16[192,256]{1,0:T(8,128)(2,1)S(1)} %fusion), channel_id=1, source_target_pairs={{0,4},{2,6},{4,0},{6,2},{1,5},{3,7},{5,1},{7,3},{8,12},{10,14},{12... | collective-permute-start | bytes 294920 | tf_op jit(solution)/shard_map/ppermute | solution.py:275

commit v6 on v5

--- a/solution.py
+++ b/solution.py
@@ -10,7 +10,8 @@
 from jax.sharding import Mesh
 from jax.sharding import PartitionSpec as P
 
-CTX = ("x", "zh", "y")
+CTX = "ctx"
+FIRST = 42
 LANES = 128
 BLOCK = 256
 CHANS = 4
@@ -18,10 +19,14 @@
 F32, BF16 = jnp.float32, jnp.bfloat16
 
 
+def order(groups):
+    return [(FIRST + rank) % groups for rank in range(groups)]
+
+
 def tables(groups):
     rows, length = 2 * groups, 2 * groups * TOKENS
-    kb = (np.arange(2)[:, None] + 2 * np.arange(groups)[None, :]).reshape(-1)
-    n1, n2 = np.arange(groups), np.arange(TOKENS)
+    n1, n2 = np.array(order(groups)), np.arange(TOKENS)
+    kb = (np.arange(2)[:, None] + 2 * n1[None, :]).reshape(-1)
     first = 2.0 * math.pi * (np.outer(n1, kb) % rows) / rows
     middle = 2.0 * math.pi * (np.outer(n2, n2) % TOKENS) / TOKENS
     turn = 2.0 * math.pi * (np.outer(kb, n2) % length) / length
@@ -232,6 +237,11 @@
     return out if many else out[0]
 
 
+def exchange(value):
+    groups = [order(lax.axis_size(CTX))]
+    return lax.all_to_all(value, CTX, 0, 0, axis_index_groups=groups, tiled=True)
+
+
 def local(query_branch, key_branch, value_branch, spectrum, skip_gain, out_weight):
     groups = lax.axis_size(CTX)
     tokens, channels = query_branch.shape
@@ -249,7 +259,7 @@
         ],
         hbm=True,
     )
-    got = lax.all_to_all(payload, CTX, 0, 0, tiled=True)
+    got = exchange(payload)
     mine, other = call(
         split_kernel,
         [(lines, channels, width)] * 2,
@@ -264,7 +274,7 @@
         (got, tables(groups)),
         [pltpu.VMEM((4, 8 * groups, LANES), F32), pltpu.VMEM((8 * groups, LANES), F32)],
     )
-    y = lax.all_to_all(y, CTX, 0, 0, tiled=True)
+    y = exchange(y)
     gated = call(
         gate_kernel,
         (tokens, channels),
@@ -290,7 +300,7 @@
 
 
 def solution(mesh):
-    fine = Mesh(mesh.devices.reshape(4, 4, 4, 4, 2), ("x", "zh", "y", "zl", "core"))
+    fine = Mesh(mesh.devices.reshape(64, 4, 2), ("ctx", "zl", "core"))
     tp = ("zl", "core")
     placed = (
         P(CTX, tp),

time: 109 us -> 98.7 us (0.906); the launches traced: 109 us -> 97.5 us
  blocking collectives: 33.3 us -> 25.4 us
  waiting for transfers between devices: 29.5 us -> 22.1 us
  starting transfers between devices: 37.5 us -> 41.3 us
    all_to_all x1, blocking collectives: 26.9 us -> 19.6 us  [exchange(): lax.all_to_all(value, CTX, 0, 0, axis_index_groups=groups, tiled=True)]
    all_to_all x1, waiting for transfers between devices: 21.7 us -> 14.7 us  [exchange(): lax.all_to_all(value, CTX, 0, 0, axis_index_groups=groups, tiled=True)]
    all_to_all x1, starting transfers between devices: 21.8 us -> 24.8 us  [exchange(): lax.all_to_all(value, CTX, 0, 0, axis_index_groups=groups, tiled=True)]
  transfers between devices with their start and end apart: 6 -> 6, of which waited for: 4 -> 4; matrix products, arithmetic and copies ran while one was open for 0% -> 0% of each run, Pallas kernels for 4% -> 5%
where the time goes in v6:
time: 98.7 us; the launch traced here: 97.5 us
  starting transfers between devices  41.3 us (42%)
  blocking collectives  25.4 us (26%)
  waiting for transfers between devices  22.1 us (22%)
  Pallas kernels  8.49 us (9%)
    all_to_all x1, starting transfers between devices, exchange(): lax.all_to_all(value, CTX, 0, 0, axis_index_groups=groups, tiled=True)  24.8 us
    all_to_all x1, blocking collectives, exchange(): lax.all_to_all(value, CTX, 0, 0, axis_index_groups=groups, tiled=True)  19.6 us
    all_to_all x1, waiting for transfers between devices, exchange(): lax.all_to_all(value, CTX, 0, 0, axis_index_groups=groups, tiled=True)  14.7 us
    ppermute x4, starting transfers between devices, trade(): return lax.ppermute(value, 'zl', [(i, i ^ d) for i in range(lines)])  13.3 us
    pallas_call x7, Pallas kernels, call(): pl.pallas_call(kernel, out_shape=out_shape, scratch_shapes=list(scratch),...  8.49 us
    ppermute x4, waiting for transfers between devices, trade(): return lax.ppermute(value, 'zl', [(i, i ^ d) for i in range(lines)])  7.35 us
    all_gather x1, blocking collectives, local(): near = lax.all_gather(gated, 'core', axis=0)  5.85 us
    ppermute x1, starting transfers between devices, local(): other = lax.ppermute(other, 'core', [(0, 1), (1, 0)])  3.27 us
  transfers between devices with their start and end apart: 6, of which 4 were waited for; matrix products, arithmetic and copies ran while one was open for 0% of the time, Pallas kernels for 5%

profile of v6, /device:TPU:1, one launch (start us, length us, event | category | flops | bytes accessed | tf_op | source)
XLA Modules:
  0.0 97.5 jit_solution(13143394559655809964)
XLA Ops:
  0.0 2.5 %shard_map.73 = (bf16[64,30,128]{2,1,0:T(8,128)(2,1)}, bf16[192,256]{1,0:T(8,128)(2,1)}) custom-call(bf16[192,256]{1,0:T(8,128)(2,1)} %k_hbm.1, bf16[192,256]{1,0:T(8,128)(2,1)} %v_hbm.1, f32[4,192,256]{2,1,0:T(8,128)} %bitcast.10), custom_call_target="tpu_custom_call" | custom-call | tf_op jit(solution)/shard_map/pallas_call | solution.py:231
  2.5 24.8 %all-to-all-start = ((bf16[64,30,128]{2,1,0:T(8,128)(2,1)}), bf16[64,30,128]{2,1,0:T(8,128)(2,1)S(1)}, u32[]{:S(2)}, u32[]{:S(2)}) async-start(bf16[64,30,128]{2,1,0:T(8,128)(2,1)} %get-tuple-element.13), calls=%async_computation | async-start | bytes 1048576 | tf_op jit(solution)/shard_map/all_to_all | solution.py:242
  27.3 0.0 copy-start.2
  27.3 0.0 copy-start.3
  27.3 0.0 copy-start.4
  27.3 3.0 %shard_map.76 = (bf16[4,256,512]{2,1,0:T(8,128)(2,1)}, bf16[4,256,512]{2,1,0:T(8,128)(2,1)}) custom-call(bf16[256,4096]{1,0:T(8,128)(2,1)} %w_hbm.1), custom_call_target="tpu_custom_call" | custom-call | tf_op jit(solution)/shard_map/pallas_call | solution.py:231
  30.3 3.3 %collective-permute-start = (bf16[4,256,512]{2,1,0:T(8,128)(2,1)}, bf16[4,256,512]{2,1,0:T(8,128)(2,1)S(1)}, u32[]{:S(2)}, u32[]{:S(2)}) collective-permute-start(bf16[4,256,512]{2,1,0:T(8,128)(2,1)} %get-tuple-element.16), channel_id=1, source_target_pairs={{0,1},{1,0},{2,3},{3,2},{4,5},{5,4},{6,7},{7,6},{8,9},{9,8},{10,11... | collective-permute-start | bytes 3145736 | tf_op jit(solution)/shard_map/ppermute | solution.py:270
  33.6 14.7 %all-to-all-done.got_ref = bf16[64,30,128]{2,1,0:T(8,128)(2,1)S(1)} async-done(((bf16[64,30,128]{2,1,0:T(8,128)(2,1)}), bf16[64,30,128]{2,1,0:T(8,128)(2,1)S(1)}, u32[]{:S(2)}, u32[]{:S(2)}) %all-to-all-start) | async-done | bytes 491552 | tf_op jit(solution)/shard_map/all_to_all | solution.py:242
  48.3 1.3 %shard_map.74 = bf16[64,6,128]{2,1,0:T(8,128)(2,1)S(1)} custom-call(bf16[64,30,128]{2,1,0:T(8,128)(2,1)S(1)} %all-to-all-done.got_ref, bf16[704,512]{1,0:T(8,128)(2,1)S(1)} %copy-done.1), custom_call_target="tpu_custom_call" | custom-call | tf_op jit(solution)/shard_map/pallas_call | solution.py:231
  49.6 19.6 %all_to_all.10.got_ref = bf16[64,6,128]{2,1,0:T(8,128)(2,1)S(1)} all-to-all(bf16[64,6,128]{2,1,0:T(8,128)(2,1)S(1)} %shard_map.74), channel_id=1, replica_groups={{336,344,352,360,368,376,384,392,400,408,416,424,432,440,448,456,464,47..., dimensions={0} | all-to-all | bytes 196608 | tf_op jit(solution)/shard_map/all_to_all | solution.py:242
  69.2 0.2 shard_map.75
  69.4 5.8 %all-gather = bf16[384,256]{1,0:T(8,128)(2,1)S(1)} all-gather(bf16[192,256]{1,0:T(8,128)(2,1)S(1)} %shard_map.75), channel_id=2, replica_groups=mesh['ctx'=64,'zl'=4,'core'=2] {'core'}, dimensions={0}, use_global_device_ids=true | all-gather | bytes 294912 | tf_op jit(solution)/shard_map/all_gather | solution.py:283
  75.3 0.0 collective-permute-done.other_ref
  75.3 0.4 shard_map.78
  75.7 4.0 %collective-permute-start.3 = (bf16[2,192,256]{2,1,0:T(8,128)(2,1)S(1)}, bf16[2,192,256]{2,1,0:T(8,128)(2,1)S(1)}, u32[]{:S(2)}, u32[]{:S(2)}) collective-permute-start(bf16[2,192,256]{2,1,0:T(8,128)(2,1)S(1)} %get-tuple-element.20), channel_id=1, source_target_pairs={{0,2},{2,0},{4,6},{6,4},{1,3},{3,1},{5,7},{7,5},{8,10},{10,8},{12,... | collective-permute-start | bytes 589832 | tf_op jit(solution)/shard_map/ppermute | solution.py:285
  79.7 0.4 shard_map.77
  80.1 1.9 %collective-permute-start.1 = (bf16[2,192,256]{2,1,0:T(8,128)(2,1)S(1)}, bf16[2,192,256]{2,1,0:T(8,128)(2,1)S(1)}, u32[]{:S(2)}, u32[]{:S(2)}) collective-permute-start(bf16[2,192,256]{2,1,0:T(8,128)(2,1)S(1)} %get-tuple-element.18), channel_id=1, source_target_pairs={{0,2},{2,0},{4,6},{6,4},{1,3},{3,1},{5,7},{7,5},{8,10},{10,8},{12,... | collective-permute-start | bytes 589832 | tf_op jit(solution)/shard_map/ppermute | solution.py:285
  82.0 2.6 %collective-permute-done.3.refs_4_ = bf16[2,192,256]{2,1,0:T(8,128)(2,1)S(1)} collective-permute-done((bf16[2,192,256]{2,1,0:T(8,128)(2,1)S(1)}, bf16[2,192,256]{2,1,0:T(8,128)(2,1)S(1)}, u32[]{:S(2)}, u32[]{:S(2)}) %collective-permute-start.3) | collective-permute-done | bytes 196640 | tf_op jit(solution)/shard_map/ppermute | solution.py:285
  84.7 3.5 %collective-permute-start.4 = (bf16[192,256]{1,0:T(8,128)(2,1)S(1)}, bf16[192,256]{1,0:T(8,128)(2,1)S(1)}, u32[]{:S(2)}, u32[]{:S(2)}) collective-permute-start(bf16[192,256]{1,0:T(8,128)(2,1)S(1)} %fusion.1), channel_id=1, source_target_pairs={{0,4},{2,6},{4,0},{6,2},{1,5},{3,7},{5,1},{7,3},{8,12},{10,14},{12... | collective-permute-start | bytes 294920 | tf_op jit(solution)/shard_map/ppermute | solution.py:285
  88.2 0.5 collective-permute-done.1.refs_1_
  88.7 3.8 %collective-permute-start.2 = (bf16[192,256]{1,0:T(8,128)(2,1)S(1)}, bf16[192,256]{1,0:T(8,128)(2,1)S(1)}, u32[]{:S(2)}, u32[]{:S(2)}) collective-permute-start(bf16[192,256]{1,0:T(8,128)(2,1)S(1)} %fusion), channel_id=1, source_target_pairs={{0,4},{2,6},{4,0},{6,2},{1,5},{3,7},{5,1},{7,3},{8,12},{10,14},{12... | collective-permute-start | bytes 294920 | tf_op jit(solution)/shard_map/ppermute | solution.py:285
  92.6 0.0 collective-permute-done.4.refs_5_
  92.6 4.2 %collective-permute-done.2.refs_2_ = bf16[192,256]{1,0:T(8,128)(2,1)S(1)} collective-permute-done((bf16[192,256]{1,0:T(8,128)(2,1)S(1)}, bf16[192,256]{1,0:T(8,128)(2,1)S(1)}, u32[]{:S(2)}, u32[]{:S(2)}) %collective-permute-start.2) | collective-permute-done | bytes 98336 | tf_op jit(solution)/shard_map/ppermute | solution.py:285
  96.8 0.7 shard_map.79
  (9 shorter events, 0.1 us)
Async XLA Ops:
  0.0 48.3 %copy-start.1 = (bf16[704,512]{1,0:T(8,128)(2,1)S(1)}, bf16[704,512]{1,0:T(8,128)(2,1)}, u32[]{:S(2)}) copy-start(bf16[704,512]{1,0:T(8,128)(2,1)} %constant.2.clone.table_ref) | copy-start | bytes 2162692
  2.5 45.8 %all-to-all-start = ((bf16[64,30,128]{2,1,0:T(8,128)(2,1)}), bf16[64,30,128]{2,1,0:T(8,128)(2,1)S(1)}, u32[]{:S(2)}, u32[]{:S(2)}) async-start(bf16[64,30,128]{2,1,0:T(8,128)(2,1)} %get-tuple-element.13), calls=%async_computation | async-start | bytes 1048576 | tf_op jit(solution)/shard_map/all_to_all | solution.py:242
  27.3 41.9 %copy-start.2 = (bf16[192,256]{1,0:T(8,128)(2,1)S(1)}, bf16[192,256]{1,0:T(8,128)(2,1)}, u32[]{:S(2)}) copy-start(bf16[192,256]{1,0:T(8,128)(2,1)} %q_ref.1) | copy-start | bytes 294916
  27.3 41.9 %copy-start.3 = (bf16[192,256]{1,0:T(8,128)(2,1)S(1)}, bf16[192,256]{1,0:T(8,128)(2,1)}, u32[]{:S(2)}) copy-start(bf16[192,256]{1,0:T(8,128)(2,1)} %get-tuple-element.14.mixed_ref) | copy-start | bytes 294916
  27.3 41.9 %copy-start.4 = (f32[256]{0:T(256)S(1)}, f32[256]{0:T(256)}, u32[]{:S(2)}) copy-start(f32[256]{0:T(256)} %param.11) | copy-start | bytes 3076
  30.3 45.0 %copy-start = (bf16[4,256,512]{2,1,0:T(8,128)(2,1)S(1)}, bf16[4,256,512]{2,1,0:T(8,128)(2,1)}, u32[]{:S(2)}) copy-start(bf16[4,256,512]{2,1,0:T(8,128)(2,1)} %get-tuple-element.15.mine_ref) | copy-start | bytes 3145732
  30.3 44.9 %collective-permute-start = (bf16[4,256,512]{2,1,0:T(8,128)(2,1)}, bf16[4,256,512]{2,1,0:T(8,128)(2,1)S(1)}, u32[]{:S(2)}, u32[]{:S(2)}) collective-permute-start(bf16[4,256,512]{2,1,0:T(8,128)(2,1)} %get-tuple-element.16), channel_id=1, source_target_pairs={{0,1},{1,0},{2,3},{3,2},{4,5},{5,4},{6,7},{7,6},{8,9},{9,8},{10,11... | collective-permute-start | bytes 3145736 | tf_op jit(solution)/shard_map/ppermute | solution.py:270
  75.7 9.0 %collective-permute-start.3 = (bf16[2,192,256]{2,1,0:T(8,128)(2,1)S(1)}, bf16[2,192,256]{2,1,0:T(8,128)(2,1)S(1)}, u32[]{:S(2)}, u32[]{:S(2)}) collective-permute-start(bf16[2,192,256]{2,1,0:T(8,128)(2,1)S(1)} %get-tuple-element.20), channel_id=1, source_target_pairs={{0,2},{2,0},{4,6},{6,4},{1,3},{3,1},{5,7},{7,5},{8,10},{10,8},{12,... | collective-permute-start | bytes 589832 | tf_op jit(solution)/shard_map/ppermute | solution.py:285
  80.1 8.6 %collective-permute-start.1 = (bf16[2,192,256]{2,1,0:T(8,128)(2,1)S(1)}, bf16[2,192,256]{2,1,0:T(8,128)(2,1)S(1)}, u32[]{:S(2)}, u32[]{:S(2)}) collective-permute-start(bf16[2,192,256]{2,1,0:T(8,128)(2,1)S(1)} %get-tuple-element.18), channel_id=1, source_target_pairs={{0,2},{2,0},{4,6},{6,4},{1,3},{3,1},{5,7},{7,5},{8,10},{10,8},{12,... | collective-permute-start | bytes 589832 | tf_op jit(solution)/shard_map/ppermute | solution.py:285
  84.7 7.9 %collective-permute-start.4 = (bf16[192,256]{1,0:T(8,128)(2,1)S(1)}, bf16[192,256]{1,0:T(8,128)(2,1)S(1)}, u32[]{:S(2)}, u32[]{:S(2)}) collective-permute-start(bf16[192,256]{1,0:T(8,128)(2,1)S(1)} %fusion.1), channel_id=1, source_target_pairs={{0,4},{2,6},{4,0},{6,2},{1,5},{3,7},{5,1},{7,3},{8,12},{10,14},{12... | collective-permute-start | bytes 294920 | tf_op jit(solution)/shard_map/ppermute | solution.py:285
  88.7 8.1 %collective-permute-start.2 = (bf16[192,256]{1,0:T(8,128)(2,1)S(1)}, bf16[192,256]{1,0:T(8,128)(2,1)S(1)}, u32[]{:S(2)}, u32[]{:S(2)}) collective-permute-start(bf16[192,256]{1,0:T(8,128)(2,1)S(1)} %fusion), channel_id=1, source_target_pairs={{0,4},{2,6},{4,0},{6,2},{1,5},{3,7},{5,1},{7,3},{8,12},{10,14},{12... | collective-permute-start | bytes 294920 | tf_op jit(solution)/shard_map/ppermute | solution.py:285

commit v7 on v6

--- a/solution.py
+++ b/solution.py
@@ -201,15 +201,15 @@
         copy.wait()
 
 
-def project_kernel(half, near_ref, mine_ref, other_ref, send_ref, keep_ref):
+def project_kernel(half, away, near_ref, mine_ref, other_ref, out_ref):
     core, line = lax.axis_index("core"), lax.axis_index("zl")
     ours, theirs = near_ref[core], near_ref[1 - core]
-    width = send_ref.shape[-1]
+    width = out_ref.shape[-1]
     columns = pl.ds(half * width, width)
-    for d, out in ((1, send_ref.at[0]), (3, send_ref.at[1]), (2, keep_ref.at[1]), (0, keep_ref.at[0])):
+    for i, d in enumerate(away):
         dest = line ^ d
         total = dot(ours, mine_ref[dest, :, columns]) + dot(theirs, other_ref[dest, :, columns])
-        out[...] = total.astype(BF16)
+        out_ref[i] = total.astype(BF16)
 
 
 def finish_kernel(*refs):
@@ -286,12 +286,12 @@
 
     parts = 2
     shape = (2, tokens, width // parts)
-    first = []
-    for half in range(parts):
-        send, keep = call(
-            functools.partial(project_kernel, half), [shape, shape], (near, mine, other)
-        )
-        first.append((keep, trade(send, 1)))
+    def project(half, away):
+        kernel = functools.partial(project_kernel, half, away)
+        return call(kernel, shape, (near, mine, other))
+
+    backs = [trade(project(half, (1, 3)), 1) for half in range(parts)]
+    first = [(project(half, (0, 2)), back) for half, back in enumerate(backs)]
     shares = []
     for keep, back in first:
         far = (keep[1].astype(F32) + back[1].astype(F32)).astype(BF16)

time: 98.7 us -> 98.6 us (level)
    pallas_call x7 -> x9, Pallas kernels: 8.49 us -> 8.81 us  [call(): pl.pallas_call(kernel, out_shape=out_shape, scratch_shapes=list(scratch),...]
where the time goes in v7:
time: 98.6 us; the launch traced here: 97.4 us
  starting transfers between devices  41.7 us (42%)
  blocking collectives  24.9 us (25%)
  waiting for transfers between devices  21.8 us (22%)
  Pallas kernels  8.81 us (9%)
    all_to_all x1, starting transfers between devices, exchange(): lax.all_to_all(value, CTX, 0, 0, axis_index_groups=groups, tiled=True)  24.8 us
    all_to_all x1, blocking collectives, exchange(): lax.all_to_all(value, CTX, 0, 0, axis_index_groups=groups, tiled=True)  19.6 us
    all_to_all x1, waiting for transfers between devices, exchange(): lax.all_to_all(value, CTX, 0, 0, axis_index_groups=groups, tiled=True)  14.7 us
    ppermute x4, starting transfers between devices, trade(): return lax.ppermute(value, 'zl', [(i, i ^ d) for i in range(lines)])  13.7 us
    pallas_call x9, Pallas kernels, call(): pl.pallas_call(kernel, out_shape=out_shape, scratch_shapes=list(scratch),...  8.81 us
    ppermute x4, waiting for transfers between devices, trade(): return lax.ppermute(value, 'zl', [(i, i ^ d) for i in range(lines)])  7.05 us
    all_gather x1, blocking collectives, local(): near = lax.all_gather(gated, 'core', axis=0)  5.26 us
    ppermute x1, starting transfers between devices, local(): other = lax.ppermute(other, 'core', [(0, 1), (1, 0)])  3.27 us
  transfers between devices with their start and end apart: 6, of which 4 were waited for; matrix products, arithmetic and copies ran while one was open for 0% of the time, Pallas kernels for 5%

profile of v7, /device:TPU:1, one launch (start us, length us, event | category | flops | bytes accessed | tf_op | source)
XLA Modules:
  0.0 97.4 jit_solution(601411319135619093)
XLA Ops:
  0.0 2.5 %shard_map.73 = (bf16[64,30,128]{2,1,0:T(8,128)(2,1)}, bf16[192,256]{1,0:T(8,128)(2,1)}) custom-call(bf16[192,256]{1,0:T(8,128)(2,1)} %k_hbm.1, bf16[192,256]{1,0:T(8,128)(2,1)} %v_hbm.1, f32[4,192,256]{2,1,0:T(8,128)} %bitcast.12), custom_call_target="tpu_custom_call" | custom-call | tf_op jit(solution)/shard_map/pallas_call | solution.py:231
  2.5 24.8 %all-to-all-start = ((bf16[64,30,128]{2,1,0:T(8,128)(2,1)}), bf16[64,30,128]{2,1,0:T(8,128)(2,1)S(1)}, u32[]{:S(2)}, u32[]{:S(2)}) async-start(bf16[64,30,128]{2,1,0:T(8,128)(2,1)} %get-tuple-element.9), calls=%async_computation | async-start | bytes 1048576 | tf_op jit(solution)/shard_map/all_to_all | solution.py:242
  27.3 0.0 copy-start.2
  27.3 0.0 copy-start.3
  27.3 0.0 copy-start.4
  27.3 3.0 %shard_map.76 = (bf16[4,256,512]{2,1,0:T(8,128)(2,1)}, bf16[4,256,512]{2,1,0:T(8,128)(2,1)}) custom-call(bf16[256,4096]{1,0:T(8,128)(2,1)} %w_hbm.1), custom_call_target="tpu_custom_call" | custom-call | tf_op jit(solution)/shard_map/pallas_call | solution.py:231
  30.3 3.3 %collective-permute-start = (bf16[4,256,512]{2,1,0:T(8,128)(2,1)}, bf16[4,256,512]{2,1,0:T(8,128)(2,1)S(1)}, u32[]{:S(2)}, u32[]{:S(2)}) collective-permute-start(bf16[4,256,512]{2,1,0:T(8,128)(2,1)} %get-tuple-element.12), channel_id=1, source_target_pairs={{0,1},{1,0},{2,3},{3,2},{4,5},{5,4},{6,7},{7,6},{8,9},{9,8},{10,11... | collective-permute-start | bytes 3145736 | tf_op jit(solution)/shard_map/ppermute | solution.py:270
  33.6 14.7 %all-to-all-done.got_ref = bf16[64,30,128]{2,1,0:T(8,128)(2,1)S(1)} async-done(((bf16[64,30,128]{2,1,0:T(8,128)(2,1)}), bf16[64,30,128]{2,1,0:T(8,128)(2,1)S(1)}, u32[]{:S(2)}, u32[]{:S(2)}) %all-to-all-start) | async-done | bytes 491552 | tf_op jit(solution)/shard_map/all_to_all | solution.py:242
  48.3 1.3 %shard_map.74 = bf16[64,6,128]{2,1,0:T(8,128)(2,1)S(1)} custom-call(bf16[64,30,128]{2,1,0:T(8,128)(2,1)S(1)} %all-to-all-done.got_ref, bf16[704,512]{1,0:T(8,128)(2,1)S(1)} %copy-done.1), custom_call_target="tpu_custom_call" | custom-call | tf_op jit(solution)/shard_map/pallas_call | solution.py:231
  49.6 19.6 %all_to_all.10.got_ref = bf16[64,6,128]{2,1,0:T(8,128)(2,1)S(1)} all-to-all(bf16[64,6,128]{2,1,0:T(8,128)(2,1)S(1)} %shard_map.74), channel_id=1, replica_groups={{336,344,352,360,368,376,384,392,400,408,416,424,432,440,448,456,464,47..., dimensions={0} | all-to-all | bytes 196608 | tf_op jit(solution)/shard_map/all_to_all | solution.py:242
  69.2 0.2 shard_map.75
  69.4 5.3 %all-gather = bf16[384,256]{1,0:T(8,128)(2,1)S(1)} all-gather(bf16[192,256]{1,0:T(8,128)(2,1)S(1)} %shard_map.75), channel_id=2, replica_groups=mesh['ctx'=64,'zl'=4,'core'=2] {'core'}, dimensions={0}, use_global_device_ids=true | all-gather | bytes 294912 | tf_op jit(solution)/shard_map/all_gather | solution.py:283
  74.7 0.3 shard_map.78
  75.0 4.6 %collective-permute-start.1 = (bf16[2,192,256]{2,1,0:T(8,128)(2,1)S(1)}, bf16[2,192,256]{2,1,0:T(8,128)(2,1)S(1)}, u32[]{:S(2)}, u32[]{:S(2)}) collective-permute-start(bf16[2,192,256]{2,1,0:T(8,128)(2,1)S(1)} %shard_map.78), channel_id=1, source_target_pairs={{0,2},{2,0},{4,6},{6,4},{1,3},{3,1},{5,7},{7,5},{8,10},{10,8},{12,... | collective-permute-start | bytes 589832 | tf_op jit(solution)/shard_map/ppermute | solution.py:285
  79.5 0.3 shard_map.80
  79.8 1.9 %collective-permute-start.3 = (bf16[2,192,256]{2,1,0:T(8,128)(2,1)S(1)}, bf16[2,192,256]{2,1,0:T(8,128)(2,1)S(1)}, u32[]{:S(2)}, u32[]{:S(2)}) collective-permute-start(bf16[2,192,256]{2,1,0:T(8,128)(2,1)S(1)} %shard_map.80), channel_id=1, source_target_pairs={{0,2},{2,0},{4,6},{6,4},{1,3},{3,1},{5,7},{7,5},{8,10},{10,8},{12,... | collective-permute-start | bytes 589832 | tf_op jit(solution)/shard_map/ppermute | solution.py:285
  81.8 0.3 shard_map.79.refs_3_
  82.0 0.3 shard_map.77.refs_0_
  82.3 2.2 %collective-permute-done.1.refs_1_ = bf16[2,192,256]{2,1,0:T(8,128)(2,1)S(1)} collective-permute-done((bf16[2,192,256]{2,1,0:T(8,128)(2,1)S(1)}, bf16[2,192,256]{2,1,0:T(8,128)(2,1)S(1)}, u32[]{:S(2)}, u32[]{:S(2)}) %collective-permute-start.1) | collective-permute-done | bytes 196640 | tf_op jit(solution)/shard_map/ppermute | solution.py:285
  84.5 3.5 %collective-permute-start.2 = (bf16[192,256]{1,0:T(8,128)(2,1)S(1)}, bf16[192,256]{1,0:T(8,128)(2,1)S(1)}, u32[]{:S(2)}, u32[]{:S(2)}) collective-permute-start(bf16[192,256]{1,0:T(8,128)(2,1)S(1)} %fusion), channel_id=1, source_target_pairs={{0,4},{2,6},{4,0},{6,2},{1,5},{3,7},{5,1},{7,3},{8,12},{10,14},{12... | collective-permute-start | bytes 294920 | tf_op jit(solution)/shard_map/ppermute | solution.py:285
  88.0 0.6 collective-permute-done.3.refs_4_
  88.6 3.7 %collective-permute-start.4 = (bf16[192,256]{1,0:T(8,128)(2,1)S(1)}, bf16[192,256]{1,0:T(8,128)(2,1)S(1)}, u32[]{:S(2)}, u32[]{:S(2)}) collective-permute-start(bf16[192,256]{1,0:T(8,128)(2,1)S(1)} %fusion.1), channel_id=1, source_target_pairs={{0,4},{2,6},{4,0},{6,2},{1,5},{3,7},{5,1},{7,3},{8,12},{10,14},{12... | collective-permute-start | bytes 294920 | tf_op jit(solution)/shard_map/ppermute | solution.py:285
  92.3 4.3 %collective-permute-done.4.refs_5_ = bf16[192,256]{1,0:T(8,128)(2,1)S(1)} collective-permute-done((bf16[192,256]{1,0:T(8,128)(2,1)S(1)}, bf16[192,256]{1,0:T(8,128)(2,1)S(1)}, u32[]{:S(2)}, u32[]{:S(2)}) %collective-permute-start.4) | collective-permute-done | bytes 98336 | tf_op jit(solution)/shard_map/ppermute | solution.py:285
  96.6 0.7 shard_map.81
  (11 shorter events, 0.1 us)
Async XLA Ops:
  0.0 48.3 %copy-start.1 = (bf16[704,512]{1,0:T(8,128)(2,1)S(1)}, bf16[704,512]{1,0:T(8,128)(2,1)}, u32[]{:S(2)}) copy-start(bf16[704,512]{1,0:T(8,128)(2,1)} %constant.2.clone.table_ref) | copy-start | bytes 2162692
  2.5 45.8 %all-to-all-start = ((bf16[64,30,128]{2,1,0:T(8,128)(2,1)}), bf16[64,30,128]{2,1,0:T(8,128)(2,1)S(1)}, u32[]{:S(2)}, u32[]{:S(2)}) async-start(bf16[64,30,128]{2,1,0:T(8,128)(2,1)} %get-tuple-element.9), calls=%async_computation | async-start | bytes 1048576 | tf_op jit(solution)/shard_map/all_to_all | solution.py:242
  27.3 41.9 %copy-start.2 = (bf16[192,256]{1,0:T(8,128)(2,1)S(1)}, bf16[192,256]{1,0:T(8,128)(2,1)}, u32[]{:S(2)}) copy-start(bf16[192,256]{1,0:T(8,128)(2,1)} %q_ref.1) | copy-start | bytes 294916
  27.3 41.9 %copy-start.3 = (bf16[192,256]{1,0:T(8,128)(2,1)S(1)}, bf16[192,256]{1,0:T(8,128)(2,1)}, u32[]{:S(2)}) copy-start(bf16[192,256]{1,0:T(8,128)(2,1)} %get-tuple-element.10.mixed_ref) | copy-start | bytes 294916
  27.3 41.9 %copy-start.4 = (f32[256]{0:T(256)S(1)}, f32[256]{0:T(256)}, u32[]{:S(2)}) copy-start(f32[256]{0:T(256)} %param.11) | copy-start | bytes 3076
  30.3 44.4 %copy-start = (bf16[4,256,512]{2,1,0:T(8,128)(2,1)S(1)}, bf16[4,256,512]{2,1,0:T(8,128)(2,1)}, u32[]{:S(2)}) copy-start(bf16[4,256,512]{2,1,0:T(8,128)(2,1)} %get-tuple-element.11.mine_ref) | copy-start | bytes 3145732
  30.3 44.4 %collective-permute-start = (bf16[4,256,512]{2,1,0:T(8,128)(2,1)}, bf16[4,256,512]{2,1,0:T(8,128)(2,1)S(1)}, u32[]{:S(2)}, u32[]{:S(2)}) collective-permute-start(bf16[4,256,512]{2,1,0:T(8,128)(2,1)} %get-tuple-element.12), channel_id=1, source_target_pairs={{0,1},{1,0},{2,3},{3,2},{4,5},{5,4},{6,7},{7,6},{8,9},{9,8},{10,11... | collective-permute-start | bytes 3145736 | tf_op jit(solution)/shard_map/ppermute | solution.py:270
  75.0 9.6 %collective-permute-start.1 = (bf16[2,192,256]{2,1,0:T(8,128)(2,1)S(1)}, bf16[2,192,256]{2,1,0:T(8,128)(2,1)S(1)}, u32[]{:S(2)}, u32[]{:S(2)}) collective-permute-start(bf16[2,192,256]{2,1,0:T(8,128)(2,1)S(1)} %shard_map.78), channel_id=1, source_target_pairs={{0,2},{2,0},{4,6},{6,4},{1,3},{3,1},{5,7},{7,5},{8,10},{10,8},{12,... | collective-permute-start | bytes 589832 | tf_op jit(solution)/shard_map/ppermute | solution.py:285
  79.8 8.8 %collective-permute-start.3 = (bf16[2,192,256]{2,1,0:T(8,128)(2,1)S(1)}, bf16[2,192,256]{2,1,0:T(8,128)(2,1)S(1)}, u32[]{:S(2)}, u32[]{:S(2)}) collective-permute-start(bf16[2,192,256]{2,1,0:T(8,128)(2,1)S(1)} %shard_map.80), channel_id=1, source_target_pairs={{0,2},{2,0},{4,6},{6,4},{1,3},{3,1},{5,7},{7,5},{8,10},{10,8},{12,... | collective-permute-start | bytes 589832 | tf_op jit(solution)/shard_map/ppermute | solution.py:285
  84.5 7.8 %collective-permute-start.2 = (bf16[192,256]{1,0:T(8,128)(2,1)S(1)}, bf16[192,256]{1,0:T(8,128)(2,1)S(1)}, u32[]{:S(2)}, u32[]{:S(2)}) collective-permute-start(bf16[192,256]{1,0:T(8,128)(2,1)S(1)} %fusion), channel_id=1, source_target_pairs={{0,4},{2,6},{4,0},{6,2},{1,5},{3,7},{5,1},{7,3},{8,12},{10,14},{12... | collective-permute-start | bytes 294920 | tf_op jit(solution)/shard_map/ppermute | solution.py:285
  88.6 8.0 %collective-permute-start.4 = (bf16[192,256]{1,0:T(8,128)(2,1)S(1)}, bf16[192,256]{1,0:T(8,128)(2,1)S(1)}, u32[]{:S(2)}, u32[]{:S(2)}) collective-permute-start(bf16[192,256]{1,0:T(8,128)(2,1)S(1)} %fusion.1), channel_id=1, source_target_pairs={{0,4},{2,6},{4,0},{6,2},{1,5},{3,7},{5,1},{7,3},{8,12},{10,14},{12... | collective-permute-start | bytes 294920 | tf_op jit(solution)/shard_map/ppermute | solution.py:285
